TPU v7x, 32 devices: a whole 2x2x4 slice. The times are simulated.
32 devices in a mesh: dp: 2 (over core), row: 4 (over z), col: 4 (over y, x).
Axes of the slice: x: 2, y: 2, z: 4, core: 2. Of those that a mesh axis runs over, the one named last changes fastest.
Arguments:
- inputs: bfloat16 [1024, 6144], P(('dp', 'row'), 'col'), may hold values from -6 to 6
- up_weight: bfloat16 [6144, 24576], P('col', ('dp', 'row')), may hold values from -0.078125 to 0.078125
- down_weight: bfloat16 [24576, 6144], P(('dp', 'row'), 'col'), may hold values from -0.0390625 to 0.0390625
- cotangent: bfloat16 [1024, 6144], P(('dp', 'row'), 'col'), may hold values from -3 to 3
Outputs:
- input_grad: bfloat16 [1024, 6144], P(('dp', 'row'), 'col')
- up_grad: bfloat16 [6144, 24576], P('col', ('dp', 'row'))
- down_grad: bfloat16 [24576, 6144], P(('dp', 'row'), 'col')
All inputs are finite; a program needn't handle non-finite values.
Results may differ from a plain program's by a relative error of at most 0.0049.
Values may be sent and summed in bfloat16 or wider, within the bound.
No kernel may reach another device: no remote copies, remote signals or barrier semaphores. Data moves between devices by JAX's collectives and lax.ppermute only.
A program may use at most 128 MiB of HBM per device.

v0:
```python
import math

import jax
import jax.numpy as jnp
from jax import lax
from jax.experimental import pallas as pl
from jax.experimental.pallas import tpu as pltpu
from jax.sharding import PartitionSpec as P

gelu_const = math.sqrt(2.0 / math.pi)
f32, b16 = jnp.float32, jnp.bfloat16


def gelu_both(value):
    square = value * value
    tangent = jnp.tanh(gelu_const * (value + 0.044715 * square * value))
    half = 0.5 * (1.0 + tangent)
    slope = half + 0.5 * value * (1.0 - tangent * tangent) * gelu_const * (1.0 + 3.0 * 0.044715 * square)
    return value * half, slope


def contract(left, right, at_left, at_right):
    return lax.dot_general(
        left, right, (((at_left,), (at_right,)), ((), ())), preferred_element_type=f32
    )


def shards(inputs, up_weight, down_weight, cotangent):
    n_row = lax.axis_size("row")
    replicas = lax.axis_size("dp")
    n_col = lax.axis_size("col")
    assert replicas == 2 and n_col == 4 and n_row % 4 == 0
    rows, width = inputs.shape
    quarter = rows // n_col
    own = lax.axis_index("col")

    def swap_x(a):
        return lax.ppermute(a, "col", [(i, i ^ 1) for i in range(n_col)])

    def swap_y(a):
        return lax.ppermute(a, "col", [(i, i ^ 2) for i in range(n_col)])

    def swap_dp(a):
        return lax.ppermute(a, "dp", [(0, 1), (1, 0)])

    def pass_row(a):
        return lax.ppermute(a, "row", [(i, (i + 1) % n_row) for i in range(n_row)])

    def reorder(a, order):
        blocks = [lax.dynamic_slice_in_dim(a, (own ^ bits) * quarter, quarter, 0) for bits in order]
        return jnp.concatenate(blocks, axis=0)

    x_outer, y_outer = (0, 2, 1, 3), (0, 1, 2, 3)

    def reorder_both():
        def body(own_ref, inputs_ref, cotangent_ref, out_ref):
            for i in range(n_col):
                for ref, order, base in ((inputs_ref, x_outer, 0), (cotangent_ref, y_outer, rows)):
                    source = pl.multiple_of((own_ref[0] ^ order[i]) * quarter, quarter)
                    out_ref[pl.ds(base + i * quarter, quarter), :] = ref[pl.ds(source, quarter), :]

        whole = pl.BlockSpec(memory_space=pltpu.VMEM)
        return pl.pallas_call(
            body,
            in_specs=[pl.BlockSpec(memory_space=pltpu.SMEM), whole, whole],
            out_specs=whole,
            out_shape=jax.ShapeDtypeStruct((2 * rows, width), b16),
            name="reorder",
        )(own.astype(jnp.int32).reshape(1), inputs, cotangent)

    if quarter % 16 == 0:
        moving = reorder_both()
    else:
        moving = jnp.concatenate([reorder(inputs, x_outer), reorder(cotangent, y_outer)], axis=0)

    group = n_row // 4
    tall = group * rows
    half = tall // 2
    work = [{} for _ in range(4)]
    blocks = {0: [moving]}

    token = ()

    def after(*values):
        tied = lax.optimization_barrier((*values, *token))[: len(values)]
        return tied if len(values) > 1 else tied[0]

    def fetch(at):
        if at > 0:
            blocks[at] = [pass_row(after(blocks[at - 1][-1]))]
        while len(blocks[at]) < group:
            blocks[at].append(pass_row(blocks[at][-1]))

    def mirror(at):
        work[at]["mine"] = jnp.stack(blocks[at])
        work[at]["other"] = swap_dp(after(work[at]["mine"]))

    def build(at):
        nonlocal token
        w = work[at]
        pair = [a.reshape(group, 2 * n_col, quarter, width) for a in after(w["mine"], w["other"])]
        both = jnp.stack([a.transpose(1, 0, 2, 3) for a in pair], axis=2).reshape(2, 2 * tall, width)
        w["in"], w["cot"] = both[0], both[1]
        token = (both,)

    def products(at, first):
        nonlocal token
        w = work[at]
        w_in, w_cot = after(w["in"], w["cot"])
        span = slice(tall, None) if first else slice(0, tall)
        hidden = contract(w_in[span], up_weight, 1, 0)
        delta_act = contract(w_cot[span], down_weight, 1, 1)
        if first:
            hidden, delta_act = hidden.astype(b16), delta_act.astype(b16)
        names = ("h_out", "g_out") if first else ("h", "g")
        w[names[0]], w[names[1]] = token = (hidden, delta_act)

    def reduce_first(at, before=()):
        w = work[at]
        h_out, g_out, *_ = after(w["h_out"], w["g_out"], *before)
        w["h_came"], w["g_came"] = swap_x(h_out), swap_y(g_out)

    def reduce_second(at):
        nonlocal token
        w = work[at]
        kept_h, kept_g, h_came, g_came = after(w["h"], w["g"], w["h_came"], w["g_came"])
        hidden, delta_act = kept_h + h_came.astype(f32), kept_g + g_came.astype(f32)
        w["h"], w["g"] = hidden[:half], delta_act[:half]
        token = (hidden[half:].astype(b16), delta_act[half:].astype(b16))
        w["h_came"], w["g_came"] = swap_y(token[0]), swap_x(token[1])

    def gather_first(at):
        nonlocal token
        w = work[at]
        kept_h, kept_g, h_came, g_came = after(w["h"], w["g"], w["h_came"], w["g_came"])
        value, slope = gelu_both(kept_h + h_came.astype(f32))
        w["active"] = value.astype(b16)
        w["delta"] = ((kept_g + g_came.astype(f32)) * slope).astype(b16)
        token = (w["delta"], w["active"])
        w["delta_came"], w["active_came"] = swap_y(w["delta"]), swap_x(w["active"])

    def join(at):
        nonlocal token
        w = work[at]
        own_d, came_d, own_a, came_a = after(w["delta"], w["delta_came"], w["active"], w["active_came"])
        w["delta"], w["active"] = token = (jnp.concatenate([own_d, came_d]), jnp.concatenate([own_a, came_a]))

    def gather_second(at):
        w = work[at]
        join(at)
        w["delta_came"], w["active_came"] = swap_x(w["delta"]), swap_y(w["active"])

    def share(at):
        nonlocal token
        w = work[at]
        parts = contract(after(w["delta"]), up_weight, 1, 1).reshape(n_col, group, 2, quarter, width)
        w["part"] = parts[:, :, 0]
        token = (parts[:, :, 1],)
        w["part_came"] = swap_dp(token[0])

    def share_sum(at):
        nonlocal token
        w = work[at]
        part, came = after(w["part"], w["part_came"])
        w["part"] = part + came
        token = (w["part"],)

    def early_grads(names):
        nonlocal token
        left, right = (jnp.concatenate(after(work[0][k], work[1][k])) for k in names)
        token = (contract(left, right, 0, 0),)
        return token[0]

    def late_grads(names, partial):
        nonlocal token
        left, right = (jnp.concatenate(after(work[2][k], work[3][k])) for k in names)
        token = (((partial + contract(left, right, 0, 0)) / replicas).astype(b16),)
        return token[0]

    def step_part(step):
        return work[step // group]["part"][:, step % group].reshape(rows, width)

    fetch(0)
    mirror(0)
    fetch(1)
    build(0)
    products(0, True)
    reduce_first(0)
    mirror(1)
    fetch(2)
    build(1)
    products(1, True)
    reduce_first(1)
    products(0, False)
    reduce_second(0)
    products(1, False)
    reduce_second(1)
    mirror(2)
    gather_first(0)
    fetch(3)
    gather_first(1)
    build(2)
    products(2, True)
    gather_second(0)
    products(2, False)
    mirror(3)
    gather_second(1)
    build(3)
    products(3, True)
    reduce_first(2, (work[0]["delta_came"], work[0]["active_came"]))
    products(3, False)
    join(0)
    reduce_first(3, (work[1]["delta_came"], work[1]["active_came"]))
    join(1)
    up_partial = early_grads(("in", "delta"))
    reduce_second(2)
    share(0)
    reduce_second(3)
    share_sum(0)
    share(1)
    gather_first(2)
    share_sum(1)
    gather_first(3)
    gather_second(2)
    gather_second(3)
    down_partial = early_grads(("active", "cot"))
    join(2)
    share(2)
    share_sum(2)
    join(3)
    share(3)
    up_grad = late_grads(("in", "delta"), up_partial)
    share_sum(3)
    down_grad = late_grads(("active", "cot"), down_partial)

    if group == 1:
        two = pass_row(step_part(1)) + step_part(2)
        two = lax.ppermute(two, "row", [(i, (i + 2) % n_row) for i in range(n_row)])
        input_grad = step_part(0) + two + pass_row(step_part(3).astype(b16)).astype(f32)
    else:
        running = pass_row(step_part(1))
        for step in range(2, n_row):
            running = pass_row(running + step_part(step))
        input_grad = step_part(0) + running
    input_grad = input_grad.astype(b16).reshape(2, 2, quarter, width).transpose(1, 0, 2, 3).reshape(rows, width)
    return (reorder(input_grad, y_outer), up_grad, down_grad)


def solution(mesh):
    tokens = P(("dp", "row"), "col")
    up, down = P("col", ("dp", "row")), P(("dp", "row"), "col")
    return jax.shard_map(
        shards,
        mesh=mesh,
        in_specs=(tokens, up, down, tokens),
        out_specs=(tokens, up, down),
        check_vma=False,
    )
```

profile of v0, /device:TPU:0, one launch (start us, length us, event | category | flops | bytes accessed | tf_op | source)
XLA Modules:
  0.0 323.2 jit_solution(429702357114294695)
XLA Ops:
  0.6 2.0 reorder.1
  3.1 2.6 collective-permute-start.1
  7.2 6.2 %convolution_convert_fusion.7 = bf16[128,3072]{1,0:T(8,128)(2,1)S(1)} fusion(bf16[1536,3072]{1,0:T(8,128)(2,1)} %param.5, bf16[256,1536]{1,0:T(8,128)(2,1)S(1)} %bitcast.111), kind=kOutput, calls=%fused_computation.9 | convolution fusion | flops 1208352768 | bytes 10616832 | tf_op jit(solution)/shard_map/dot_general | solution.py:23
  13.4 4.0 %convolution_convert_fusion.6 = bf16[128,3072]{1,0:T(8,128)(2,1)} fusion(bf16[3072,1536]{1,0:T(8,128)(2,1)S(1)} %copy-done, bf16[256,1536]{1,0:T(8,128)(2,1)S(1)} %bitcast.117), kind=kOutput, calls=%fused_computation.8 | convolution fusion | flops 1208352768 | bytes 10616832 | tf_op jit(solution)/shard_map/dot_general | solution.py:23
  17.5 8.8 %collective-permute-done.1 = bf16[256,1536]{1,0:T(8,128)(2,1)} collective-permute-done((bf16[256,1536]{1,0:T(8,128)(2,1)}, bf16[256,1536]{1,0:T(8,128)(2,1)}, u32[]{:S(2)}, u32[]{:S(2)}) %collective-permute-start.1) | collective-permute-done | bytes 786464 | tf_op jit(solution)/shard_map/ppermute | solution.py:47
  27.8 1.5 collective-permute-start.4
  31.1 2.3 convolution_convert_fusion.5
  33.4 4.1 %convolution_convert_fusion.4 = bf16[128,3072]{1,0:T(8,128)(2,1)} fusion(bf16[3072,1536]{1,0:T(8,128)(2,1)S(1)} %copy-done, bf16[256,1536]{1,0:T(8,128)(2,1)S(1)} %bitcast.123), kind=kOutput, calls=%fused_computation.6 | convolution fusion | flops 1208352768 | bytes 10616832 | tf_op jit(solution)/shard_map/dot_general | solution.py:23
  37.5 1.6 fusion.58
  39.1 3.1 fusion.56
  42.2 4.2 %collective-permute-done.3 = bf16[128,3072]{1,0:T(8,128)(2,1)} collective-permute-done((bf16[128,3072]{1,0:T(8,128)(2,1)S(1)}, bf16[128,3072]{1,0:T(8,128)(2,1)}, u32[]{:S(2)}, u32[]{:S(2)}) %collective-permute-start.3) | collective-permute-done | bytes 786464 | tf_op jit(solution)/shard_map/ppermute | solution.py:38
  57.6 3.1 fusion.52
  60.7 20.2 %collective-permute-done.7 = bf16[128,3072]{1,0:T(8,128)(2,1)S(1)} collective-permute-done((bf16[128,3072]{1,0:T(8,128)(2,1)}, bf16[128,3072]{1,0:T(8,128)(2,1)S(1)}, u32[]{:S(2)}, u32[]{:S(2)}) %collective-permute-start.7) | collective-permute-done | bytes 786464 | tf_op jit(solution)/shard_map/ppermute | solution.py:38
  83.0 1.6 multiply_convert_fusion.8
  87.5 5.8 %collective-permute-done.13 = bf16[64,3072]{1,0:T(8,128)(2,1)S(1)} collective-permute-done((bf16[64,3072]{1,0:T(8,128)(2,1)S(1)}, bf16[64,3072]{1,0:T(8,128)(2,1)S(1)}, u32[]{:S(2)}, u32[]{:S(2)}) %collective-permute-start.13) | collective-permute-done | bytes 393248 | tf_op jit(solution)/shard_map/ppermute | solution.py:41
  94.1 2.2 collective-permute-start.19
  97.6 2.3 convolution_convert_fusion.3
  99.9 4.1 %convolution_convert_fusion.2 = bf16[128,3072]{1,0:T(8,128)(2,1)} fusion(bf16[3072,1536]{1,0:T(8,128)(2,1)S(1)} %copy-done, bf16[256,1536]{1,0:T(8,128)(2,1)S(1)} %bitcast.120), kind=kOutput, calls=%fused_computation.4 | convolution fusion | flops 1208352768 | bytes 10616832 | tf_op jit(solution)/shard_map/dot_general | solution.py:23
  106.3 2.0 collective-permute-start.15
  110.6 3.1 fusion.46
  114.5 1.8 constant_dynamic-update-slice_fusion.4
  117.9 1.9 collective-permute-start.24
  119.9 2.4 convolution_convert_fusion.1
  122.3 4.0 %convolution_convert_fusion = bf16[128,3072]{1,0:T(8,128)(2,1)} fusion(bf16[3072,1536]{1,0:T(8,128)(2,1)S(1)} %copy-done, bf16[256,1536]{1,0:T(8,128)(2,1)S(1)} %bitcast.126), kind=kOutput, calls=%fused_computation.2 | convolution fusion | flops 1208352768 | bytes 10616832 | tf_op jit(solution)/shard_map/dot_general | solution.py:23
  127.8 4.3 %fusion.40 = f32[128,3072]{1,0:T(8,128)S(1)} fusion(bf16[3072,1536]{1,0:T(8,128)(2,1)S(1)} %copy-done, bf16[256,1536]{1,0:T(8,128)(2,1)} %bitcast.127), kind=kOutput, calls=%fused_computation.109 | convolution fusion | flops 1207959552 | bytes 11403264 | tf_op jit(solution)/shard_map/dot_general | solution.py:23
  136.0 5.7 %collective-permute-done.23 = bf16[128,3072]{1,0:T(8,128)(2,1)} collective-permute-done((bf16[128,3072]{1,0:T(8,128)(2,1)}, bf16[128,3072]{1,0:T(8,128)(2,1)}, u32[]{:S(2)}, u32[]{:S(2)}) %collective-permute-start.23) | collective-permute-done | bytes 786464 | tf_op jit(solution)/shard_map/ppermute | solution.py:38
  142.9 2.2 constant_dynamic-update-slice_fusion.15
  147.6 2.1 constant_dynamic-update-slice_fusion.14
  153.8 10.4 %fusion = f32[1536,3072]{1,0:T(8,128)} fusion(bf16[256,3072]{1,0:T(8,128)(2,1)} %copy-done.31, bf16[256,3072]{1,0:T(8,128)(2,1)S(1)} %get-tuple-element.207, bf16[256,1536]{1,0:T(8,128)(2,1)S(1)} %bitcast.116, bf16[256,1536]{1,0:T(8,128)(2,1)S(1)} %bitcast.113), kind=kOutput, calls=%fused_computation.10 | convolution fusion | flops 4841275392 | bytes 23592960 | tf_op jit(solution)/shard_map/dot_general | solution.py:23
  164.2 6.0 %collective-permute-done.21 = bf16[128,3072]{1,0:T(8,128)(2,1)S(1)} collective-permute-done((bf16[128,3072]{1,0:T(8,128)(2,1)S(1)}, bf16[128,3072]{1,0:T(8,128)(2,1)S(1)}, u32[]{:S(2)}, u32[]{:S(2)}) %collective-permute-start.21) | collective-permute-done | bytes 786464 | tf_op jit(solution)/shard_map/ppermute | solution.py:38
  175.2 2.6 fusion.68
  178.0 9.0 %collective-permute-done.26 = bf16[128,3072]{1,0:T(8,128)(2,1)S(1)} collective-permute-done((bf16[128,3072]{1,0:T(8,128)(2,1)S(1)}, bf16[128,3072]{1,0:T(8,128)(2,1)S(1)}, u32[]{:S(2)}, u32[]{:S(2)}) %collective-permute-start.26) | collective-permute-done | bytes 786464 | tf_op jit(solution)/shard_map/ppermute | solution.py:38
  188.1 2.1 copy-done.32
  190.3 2.6 fusion.69
  193.2 1.5 collective-permute-start.34
  199.2 6.0 %collective-permute-done.34 = bf16[64,3072]{1,0:T(8,128)(2,1)S(1)} collective-permute-done((bf16[64,3072]{1,0:T(8,128)(2,1)S(1)}, bf16[64,3072]{1,0:T(8,128)(2,1)S(1)}, u32[]{:S(2)}, u32[]{:S(2)}) %collective-permute-start.34) | collective-permute-done | bytes 393248 | tf_op jit(solution)/shard_map/ppermute | solution.py:41
  209.4 4.2 %collective-permute-done.32 = bf16[64,3072]{1,0:T(8,128)(2,1)S(1)} collective-permute-done((bf16[64,3072]{1,0:T(8,128)(2,1)S(1)}, bf16[64,3072]{1,0:T(8,128)(2,1)S(1)}, u32[]{:S(2)}, u32[]{:S(2)}) %collective-permute-start.32) | collective-permute-done | bytes 393248 | tf_op jit(solution)/shard_map/ppermute | solution.py:41
  215.2 1.6 collective-permute-start.36
  217.4 4.6 %collective-permute-done.38 = bf16[64,3072]{1,0:T(8,128)(2,1)S(1)} collective-permute-done((bf16[64,3072]{1,0:T(8,128)(2,1)S(1)}, bf16[64,3072]{1,0:T(8,128)(2,1)S(1)}, u32[]{:S(2)}, u32[]{:S(2)}) %collective-permute-start.38) | collective-permute-done | bytes 393248 | tf_op jit(solution)/shard_map/ppermute | solution.py:41
  225.2 11.0 %fusion.4 = f32[3072,1536]{1,0:T(8,128)} fusion(bf16[256,3072]{1,0:T(8,128)(2,1)} %constant_dynamic-update-slice_fusion.14, bf16[256,3072]{1,0:T(8,128)(2,1)S(1)} %copy-done.29, bf16[256,1536]{1,0:T(8,128)(2,1)S(1)} %bitcast.125, bf16[256,1536]{1,0:T(8,128)(2,1)S(1)} %bitcast.119), kind=kOutput, calls=%fused_computation.14 | convolution fusion | flops 4841275392 | bytes 23592960 | tf_op jit(solution)/shard_map/dot_general | solution.py:23
  236.2 3.4 %collective-permute-done.36 = bf16[128,3072]{1,0:T(8,128)(2,1)S(1)} collective-permute-done((bf16[128,3072]{1,0:T(8,128)(2,1)S(1)}, bf16[128,3072]{1,0:T(8,128)(2,1)S(1)}, u32[]{:S(2)}, u32[]{:S(2)}) %collective-permute-start.36) | collective-permute-done | bytes 786464 | tf_op jit(solution)/shard_map/ppermute | solution.py:38
  239.9 2.6 fusion.70
  247.5 16.4 %collective-permute-done.42 = bf16[128,3072]{1,0:T(8,128)(2,1)} collective-permute-done((bf16[128,3072]{1,0:T(8,128)(2,1)}, bf16[128,3072]{1,0:T(8,128)(2,1)}, u32[]{:S(2)}, u32[]{:S(2)}) %collective-permute-start.42) | collective-permute-done | bytes 786464 | tf_op jit(solution)/shard_map/ppermute | solution.py:38
  268.2 2.7 constant_dynamic-update-slice_fusion.30
  270.9 5.4 %fusion.71 = f32[256,1536]{1,0:T(8,128)S(1)} fusion(bf16[256,3072]{1,0:T(8,128)(2,1)S(1)} %constant_dynamic-update-slice_fusion.28, bf16[1536,3072]{1,0:T(8,128)(2,1)} %param.5), kind=kOutput, calls=%fused_computation.176 | convolution fusion | flops 2415919104 | bytes 12582912 | tf_op jit(solution)/shard_map/dot_general | solution.py:23
  277.8 12.1 %multiply_convert_fusion.1 = bf16[1536,3072]{1,0:T(8,128)(2,1)} fusion(f32[1536,3072]{1,0:T(8,128)} %fusion, bf16[256,3072]{1,0:T(8,128)(2,1)} %copy-done.34, bf16[256,3072]{1,0:T(8,128)(2,1)} %copy-done.33, bf16[256,1536]{1,0:T(8,128)(2,1)S(1)} %bitcast.110, bf16[256,1536]{1,0:T(8,128)(2,1)S(1)} %bitcast.107), kind=kOutput, calls=%fused_computation.1 | convolution fusion | flops 4855431168 | bytes 33030144 | tf_op jit(solution)/shard_map/dot_general | solution.py:23
  291.4 12.3 %multiply_convert_fusion = bf16[3072,1536]{1,0:T(8,128)(2,1)} fusion(f32[3072,1536]{1,0:T(8,128)} %fusion.4, bf16[256,3072]{1,0:T(8,128)(2,1)} %constant_dynamic-update-slice_fusion.30, bf16[256,3072]{1,0:T(8,128)(2,1)} %copy-done.30, bf16[256,1536]{1,0:T(8,128)(2,1)S(1)} %bitcast.128, bf16[256,1536]{1,0:T(8,128)(2,1)S(1)} %bitcast.122), kind=kOutput, calls=%fused_computation | convolution fusion | flops 4855431168 | bytes 33030144 | tf_op jit(solution)/shard_map/dot_general | solution.py:23
  303.7 18.3 %collective-permute-done.41 = f32[128,1536]{1,0:T(8,128)S(1)} collective-permute-done((f32[128,1536]{1,0:T(8,128)S(1)}, f32[128,1536]{1,0:T(8,128)S(1)}, u32[]{:S(2)}, u32[]{:S(2)}) %collective-permute-start.41) | collective-permute-done | bytes 786464 | tf_op jit(solution)/shard_map/ppermute | solution.py:238
  (229 shorter events, 77.2 us)
Async XLA Ops:
  2.7 3.0 collective-permute-start
  3.1 23.1 %collective-permute-start.1 = (bf16[256,1536]{1,0:T(8,128)(2,1)}, bf16[256,1536]{1,0:T(8,128)(2,1)}, u32[]{:S(2)}, u32[]{:S(2)}) collective-permute-start(bf16[256,1536]{1,0:T(8,128)(2,1)} %reorder.1), channel_id=1, source_target_pairs={{0,4},{4,8},{8,12},{12,0},{1,5},{5,9},{9,13},{13,1},{2,6},{6,10},{... | collective-permute-start | bytes 2359304 | tf_op jit(solution)/shard_map/ppermute | solution.py:47
  7.1 30.4 %copy-start.5 = (bf16[4,1,2,32,1536]{4,3,2,0,1:T(8,128)(2,1)}, bf16[4,1,2,32,1536]{4,3,2,0,1:T(8,128)(2,1)S(1)}, u32[]{:S(2)}) copy-start(bf16[4,1,2,32,1536]{4,3,2,0,1:T(8,128)(2,1)S(1)} %get-tuple-element.276) | copy-start | bytes 2359300
  7.1 31.9 %copy-start.16 = (bf16[4,1,2,32,1536]{4,3,2,0,1:T(8,128)(2,1)}, bf16[4,1,2,32,1536]{4,3,2,0,1:T(8,128)(2,1)S(1)}, u32[]{:S(2)}) copy-start(bf16[4,1,2,32,1536]{4,3,2,0,1:T(8,128)(2,1)S(1)} %get-tuple-element.275) | copy-start | bytes 2359300
  26.3 3.5 %collective-permute-start.2 = (bf16[1,256,1536]{2,1,0:T(8,128)(2,1)}, bf16[1,256,1536]{2,1,0:T(8,128)(2,1)S(1)}, u32[]{:S(2)}, u32[]{:S(2)}) collective-permute-start(bf16[1,256,1536]{2,1,0:T(8,128)(2,1)} %bitcast.8), channel_id=1, source_target_pairs={{0,16},{16,0},{1,17},{17,1},{2,18},{18,2},{3,19},{19,3},{4,20},{20... | collective-permute-start | bytes 2359304 | tf_op jit(solution)/shard_map/ppermute | solution.py:44
  26.3 20.1 %collective-permute-start.3 = (bf16[128,3072]{1,0:T(8,128)(2,1)S(1)}, bf16[128,3072]{1,0:T(8,128)(2,1)}, u32[]{:S(2)}, u32[]{:S(2)}) collective-permute-start(bf16[128,3072]{1,0:T(8,128)(2,1)S(1)} %convolution_convert_fusion.7), channel_id=1, source_target_pairs={{0,1},{1,0},{2,3},{3,2},{4,5},{5,4},{6,7},{7,6},{8,9},{9,8},{10,11... | collective-permute-start | bytes 2359304 | tf_op jit(solution)/shard_map/ppermute | solution.py:38
  27.8 20.0 %collective-permute-start.4 = (bf16[128,3072]{1,0:T(8,128)(2,1)}, bf16[128,3072]{1,0:T(8,128)(2,1)}, u32[]{:S(2)}, u32[]{:S(2)}) collective-permute-start(bf16[128,3072]{1,0:T(8,128)(2,1)} %convolution_convert_fusion.6), channel_id=1, source_target_pairs={{0,2},{1,3},{2,0},{3,1},{4,6},{5,7},{6,4},{7,5},{8,10},{9,11},{10,... | collective-permute-start | bytes 2359304 | tf_op jit(solution)/shard_map/ppermute | solution.py:41
  29.3 53.3 %collective-permute-start.11 = (bf16[256,1536]{1,0:T(8,128)(2,1)}, bf16[256,1536]{1,0:T(8,128)(2,1)}, u32[]{:S(2)}, u32[]{:S(2)}) collective-permute-start(bf16[256,1536]{1,0:T(8,128)(2,1)} %collective-permute-done.1), channel_id=1, source_target_pairs={{0,4},{4,8},{8,12},{12,0},{1,5},{5,9},{9,13},{13,1},{2,6},{6,10},{... | collective-permute-start | bytes 2359304 | tf_op jit(solution)/shard_map/ppermute | solution.py:47
  52.2 30.4 %collective-permute-start.5 = (bf16[64,3072]{1,0:T(8,128)(2,1)}, bf16[64,3072]{1,0:T(8,128)(2,1)S(1)}, u32[]{:S(2)}, u32[]{:S(2)}) collective-permute-start(bf16[64,3072]{1,0:T(8,128)(2,1)} %slice.319), channel_id=1, source_target_pairs={{0,2},{1,3},{2,0},{3,1},{4,6},{5,7},{6,4},{7,5},{8,10},{9,11},{10,... | collective-permute-start | bytes 1179656 | tf_op jit(solution)/shard_map/ppermute | solution.py:41
  53.7 28.9 %collective-permute-start.6 = (bf16[64,3072]{1,0:T(8,128)(2,1)}, bf16[64,3072]{1,0:T(8,128)(2,1)}, u32[]{:S(2)}, u32[]{:S(2)}) collective-permute-start(bf16[64,3072]{1,0:T(8,128)(2,1)} %slice.318), channel_id=1, source_target_pairs={{0,1},{1,0},{2,3},{3,2},{4,5},{5,4},{6,7},{7,6},{8,9},{9,8},{10,11... | collective-permute-start | bytes 1179656 | tf_op jit(solution)/shard_map/ppermute | solution.py:38
  54.2 26.7 %collective-permute-start.7 = (bf16[128,3072]{1,0:T(8,128)(2,1)}, bf16[128,3072]{1,0:T(8,128)(2,1)S(1)}, u32[]{:S(2)}, u32[]{:S(2)}) collective-permute-start(bf16[128,3072]{1,0:T(8,128)(2,1)} %convolution_convert_fusion.5), channel_id=1, source_target_pairs={{0,1},{1,0},{2,3},{3,2},{4,5},{5,4},{6,7},{7,6},{8,9},{9,8},{10,11... | collective-permute-start | bytes 2359304 | tf_op jit(solution)/shard_map/ppermute | solution.py:38
  55.7 25.2 %collective-permute-start.8 = (bf16[128,3072]{1,0:T(8,128)(2,1)}, bf16[128,3072]{1,0:T(8,128)(2,1)S(1)}, u32[]{:S(2)}, u32[]{:S(2)}) collective-permute-start(bf16[128,3072]{1,0:T(8,128)(2,1)} %convolution_convert_fusion.4), channel_id=1, source_target_pairs={{0,2},{1,3},{2,0},{3,1},{4,6},{5,7},{6,4},{7,5},{8,10},{9,11},{10,... | collective-permute-start | bytes 2359304 | tf_op jit(solution)/shard_map/ppermute | solution.py:41
  81.2 12.1 %collective-permute-start.13 = (bf16[64,3072]{1,0:T(8,128)(2,1)S(1)}, bf16[64,3072]{1,0:T(8,128)(2,1)S(1)}, u32[]{:S(2)}, u32[]{:S(2)}) collective-permute-start(bf16[64,3072]{1,0:T(8,128)(2,1)S(1)} %slice.317), channel_id=1, source_target_pairs={{0,2},{1,3},{2,0},{3,1},{4,6},{5,7},{6,4},{7,5},{8,10},{9,11},{10,... | collective-permute-start | bytes 1179656 | tf_op jit(solution)/shard_map/ppermute | solution.py:41
  82.0 11.5 %collective-permute-start.14 = (bf16[64,3072]{1,0:T(8,128)(2,1)S(1)}, bf16[64,3072]{1,0:T(8,128)(2,1)S(1)}, u32[]{:S(2)}, u32[]{:S(2)}) collective-permute-start(bf16[64,3072]{1,0:T(8,128)(2,1)S(1)} %slice.316), channel_id=1, source_target_pairs={{0,1},{1,0},{2,3},{3,2},{4,5},{5,4},{6,7},{7,6},{8,9},{9,8},{10,11... | collective-permute-start | bytes 1179656 | tf_op jit(solution)/shard_map/ppermute | solution.py:38
  82.6 13.7 %collective-permute-start.12 = (bf16[1,256,1536]{2,1,0:T(8,128)(2,1)}, bf16[1,256,1536]{2,1,0:T(8,128)(2,1)S(1)}, u32[]{:S(2)}, u32[]{:S(2)}) collective-permute-start(bf16[1,256,1536]{2,1,0:T(8,128)(2,1)} %bitcast.15), channel_id=1, source_target_pairs={{0,16},{16,0},{1,17},{17,1},{2,18},{18,2},{3,19},{19,3},{4,20},{20... | collective-permute-start | bytes 2359304 | tf_op jit(solution)/shard_map/ppermute | solution.py:44
  84.7 19.2 %collective-permute-start.9 = (bf16[64,3072]{1,0:T(8,128)(2,1)S(1)}, bf16[64,3072]{1,0:T(8,128)(2,1)S(1)}, u32[]{:S(2)}, u32[]{:S(2)}) collective-permute-start(bf16[64,3072]{1,0:T(8,128)(2,1)S(1)} %get-tuple-element.171), channel_id=1, source_target_pairs={{0,2},{1,3},{2,0},{3,1},{4,6},{5,7},{6,4},{7,5},{8,10},{9,11},{10,... | collective-permute-start | bytes 1179656 | tf_op jit(solution)/shard_map/ppermute | solution.py:41
  86.0 18.0 %collective-permute-start.10 = (bf16[64,3072]{1,0:T(8,128)(2,1)S(1)}, bf16[64,3072]{1,0:T(8,128)(2,1)S(1)}, u32[]{:S(2)}, u32[]{:S(2)}) collective-permute-start(bf16[64,3072]{1,0:T(8,128)(2,1)S(1)} %get-tuple-element.173), channel_id=1, source_target_pairs={{0,1},{1,0},{2,3},{3,2},{4,5},{5,4},{6,7},{7,6},{8,9},{9,8},{10,11... | collective-permute-start | bytes 1179656 | tf_op jit(solution)/shard_map/ppermute | solution.py:38
  93.3 21.2 %collective-permute-start.17 = (bf16[256,1536]{1,0:T(8,128)(2,1)}, bf16[256,1536]{1,0:T(8,128)(2,1)S(1)}, u32[]{:S(2)}, u32[]{:S(2)}) collective-permute-start(bf16[256,1536]{1,0:T(8,128)(2,1)} %collective-permute-done.11), channel_id=1, source_target_pairs={{0,4},{4,8},{8,12},{12,0},{1,5},{5,9},{9,13},{13,1},{2,6},{6,10},{... | collective-permute-start | bytes 2359304 | tf_op jit(solution)/shard_map/ppermute | solution.py:47
  94.1 19.6 %collective-permute-start.19 = (bf16[64,3072]{1,0:T(8,128)(2,1)S(1)}, bf16[64,3072]{1,0:T(8,128)(2,1)}, u32[]{:S(2)}, u32[]{:S(2)}) collective-permute-start(bf16[64,3072]{1,0:T(8,128)(2,1)S(1)} %get-tuple-element.179), channel_id=1, source_target_pairs={{0,2},{1,3},{2,0},{3,1},{4,6},{5,7},{6,4},{7,5},{8,10},{9,11},{10,... | collective-permute-start | bytes 1179656 | tf_op jit(solution)/shard_map/ppermute | solution.py:41
  96.3 17.4 %collective-permute-start.20 = (bf16[64,3072]{1,0:T(8,128)(2,1)S(1)}, bf16[64,3072]{1,0:T(8,128)(2,1)S(1)}, u32[]{:S(2)}, u32[]{:S(2)}) collective-permute-start(bf16[64,3072]{1,0:T(8,128)(2,1)S(1)} %get-tuple-element.181), channel_id=1, source_target_pairs={{0,1},{1,0},{2,3},{3,2},{4,5},{5,4},{6,7},{7,6},{8,9},{9,8},{10,11... | collective-permute-start | bytes 1179656 | tf_op jit(solution)/shard_map/ppermute | solution.py:38
  106.3 25.8 %collective-permute-start.15 = (bf16[128,3072]{1,0:T(8,128)(2,1)}, bf16[128,3072]{1,0:T(8,128)(2,1)}, u32[]{:S(2)}, u32[]{:S(2)}) collective-permute-start(bf16[128,3072]{1,0:T(8,128)(2,1)} %constant_dynamic-update-slice_fusion), channel_id=1, source_target_pairs={{0,1},{1,0},{2,3},{3,2},{4,5},{5,4},{6,7},{7,6},{8,9},{9,8},{10,11... | collective-permute-start | bytes 2359304 | tf_op jit(solution)/shard_map/ppermute | solution.py:38
  109.1 23.0 %collective-permute-start.16 = (bf16[128,3072]{1,0:T(8,128)(2,1)}, bf16[128,3072]{1,0:T(8,128)(2,1)}, u32[]{:S(2)}, u32[]{:S(2)}) collective-permute-start(bf16[128,3072]{1,0:T(8,128)(2,1)} %constant_dynamic-update-slice_fusion.2), channel_id=1, source_target_pairs={{0,2},{1,3},{2,0},{3,1},{4,6},{5,7},{6,4},{7,5},{8,10},{9,11},{10,... | collective-permute-start | bytes 2359304 | tf_op jit(solution)/shard_map/ppermute | solution.py:41
  114.5 5.3 %collective-permute-start.18 = (bf16[1,256,1536]{2,1,0:T(8,128)(2,1)S(1)}, bf16[1,256,1536]{2,1,0:T(8,128)(2,1)S(1)}, u32[]{:S(2)}, u32[]{:S(2)}) collective-permute-start(bf16[1,256,1536]{2,1,0:T(8,128)(2,1)S(1)} %bitcast.138), channel_id=1, source_target_pairs={{0,16},{16,0},{1,17},{17,1},{2,18},{18,2},{3,19},{19,3},{4,20},{20... | collective-permute-start | bytes 2359304 | tf_op jit(solution)/shard_map/ppermute | solution.py:44
  116.2 25.5 %collective-permute-start.23 = (bf16[128,3072]{1,0:T(8,128)(2,1)}, bf16[128,3072]{1,0:T(8,128)(2,1)}, u32[]{:S(2)}, u32[]{:S(2)}) collective-permute-start(bf16[128,3072]{1,0:T(8,128)(2,1)} %constant_dynamic-update-slice_fusion.4), channel_id=1, source_target_pairs={{0,1},{1,0},{2,3},{3,2},{4,5},{5,4},{6,7},{7,6},{8,9},{9,8},{10,11... | collective-permute-start | bytes 2359304 | tf_op jit(solution)/shard_map/ppermute | solution.py:38
  117.9 23.8 %collective-permute-start.24 = (bf16[128,3072]{1,0:T(8,128)(2,1)}, bf16[128,3072]{1,0:T(8,128)(2,1)}, u32[]{:S(2)}, u32[]{:S(2)}) collective-permute-start(bf16[128,3072]{1,0:T(8,128)(2,1)} %constant_dynamic-update-slice_fusion.6), channel_id=1, source_target_pairs={{0,2},{1,3},{2,0},{3,1},{4,6},{5,7},{6,4},{7,5},{8,10},{9,11},{10,... | collective-permute-start | bytes 2359304 | tf_op jit(solution)/shard_map/ppermute | solution.py:41
  149.7 20.5 %collective-permute-start.21 = (bf16[128,3072]{1,0:T(8,128)(2,1)S(1)}, bf16[128,3072]{1,0:T(8,128)(2,1)S(1)}, u32[]{:S(2)}, u32[]{:S(2)}) collective-permute-start(bf16[128,3072]{1,0:T(8,128)(2,1)S(1)} %copy-done.24), channel_id=1, source_target_pairs={{0,1},{1,0},{2,3},{3,2},{4,5},{5,4},{6,7},{7,6},{8,9},{9,8},{10,11... | collective-permute-start | bytes 2359304 | tf_op jit(solution)/shard_map/ppermute | solution.py:38
  150.2 20.5 %collective-permute-start.22 = (bf16[128,3072]{1,0:T(8,128)(2,1)S(1)}, bf16[128,3072]{1,0:T(8,128)(2,1)S(1)}, u32[]{:S(2)}, u32[]{:S(2)}) collective-permute-start(bf16[128,3072]{1,0:T(8,128)(2,1)S(1)} %copy-done.26), channel_id=1, source_target_pairs={{0,2},{1,3},{2,0},{3,1},{4,6},{5,7},{6,4},{7,5},{8,10},{9,11},{10,... | collective-permute-start | bytes 2359304 | tf_op jit(solution)/shard_map/ppermute | solution.py:41
  151.7 35.3 %collective-permute-start.26 = (bf16[128,3072]{1,0:T(8,128)(2,1)S(1)}, bf16[128,3072]{1,0:T(8,128)(2,1)S(1)}, u32[]{:S(2)}, u32[]{:S(2)}) collective-permute-start(bf16[128,3072]{1,0:T(8,128)(2,1)S(1)} %copy-done.25), channel_id=1, source_target_pairs={{0,1},{1,0},{2,3},{3,2},{4,5},{5,4},{6,7},{7,6},{8,9},{9,8},{10,11... | collective-permute-start | bytes 2359304 | tf_op jit(solution)/shard_map/ppermute | solution.py:38
  153.2 34.4 %collective-permute-start.27 = (bf16[128,3072]{1,0:T(8,128)(2,1)S(1)}, bf16[128,3072]{1,0:T(8,128)(2,1)S(1)}, u32[]{:S(2)}, u32[]{:S(2)}) collective-permute-start(bf16[128,3072]{1,0:T(8,128)(2,1)S(1)} %copy-done.27), channel_id=1, source_target_pairs={{0,2},{1,3},{2,0},{3,1},{4,6},{5,7},{6,4},{7,5},{8,10},{9,11},{10,... | collective-permute-start | bytes 2359304 | tf_op jit(solution)/shard_map/ppermute | solution.py:41
  172.2 24.0 %collective-permute-start.29 = (bf16[64,3072]{1,0:T(8,128)(2,1)S(1)}, bf16[64,3072]{1,0:T(8,128)(2,1)S(1)}, u32[]{:S(2)}, u32[]{:S(2)}) collective-permute-start(bf16[64,3072]{1,0:T(8,128)(2,1)S(1)} %slice.315), channel_id=1, source_target_pairs={{0,2},{1,3},{2,0},{3,1},{4,6},{5,7},{6,4},{7,5},{8,10},{9,11},{10,... | collective-permute-start | bytes 1179656 | tf_op jit(solution)/shard_map/ppermute | solution.py:41
  173.7 22.5 %collective-permute-start.30 = (bf16[64,3072]{1,0:T(8,128)(2,1)}, bf16[64,3072]{1,0:T(8,128)(2,1)S(1)}, u32[]{:S(2)}, u32[]{:S(2)}) collective-permute-start(bf16[64,3072]{1,0:T(8,128)(2,1)} %slice.314), channel_id=1, source_target_pairs={{0,1},{1,0},{2,3},{3,2},{4,5},{5,4},{6,7},{7,6},{8,9},{9,8},{10,11... | collective-permute-start | bytes 1179656 | tf_op jit(solution)/shard_map/ppermute | solution.py:38
  178.0 10.1 %collective-permute-start.25 = (f32[4,1,32,1536]{3,2,0,1:T(8,128)S(1)}, f32[4,1,32,1536]{3,2,0,1:T(8,128)S(1)}, u32[]{:S(2)}, u32[]{:S(2)}) collective-permute-start(f32[4,1,32,1536]{3,2,0,1:T(8,128)S(1)} %get-tuple-element.267), channel_id=1, source_target_pairs={{0,16},{16,0},{1,17},{17,1},{2,18},{18,2},{3,19},{19,3},{4,20},{20... | collective-permute-start | bytes 2359304 | tf_op jit(solution)/shard_map/ppermute | solution.py:44
  193.0 5.2 %collective-permute-start.28 = (f32[4,1,32,1536]{3,2,0,1:T(8,128)S(1)}, f32[4,1,32,1536]{3,2,0,1:T(8,128)S(1)}, u32[]{:S(2)}, u32[]{:S(2)}) collective-permute-start(f32[4,1,32,1536]{3,2,0,1:T(8,128)S(1)} %get-tuple-element.265), channel_id=1, source_target_pairs={{0,16},{16,0},{1,17},{17,1},{2,18},{18,2},{3,19},{19,3},{4,20},{20... | collective-permute-start | bytes 2359304 | tf_op jit(solution)/shard_map/ppermute | solution.py:44
  193.2 12.0 %collective-permute-start.34 = (bf16[64,3072]{1,0:T(8,128)(2,1)S(1)}, bf16[64,3072]{1,0:T(8,128)(2,1)S(1)}, u32[]{:S(2)}, u32[]{:S(2)}) collective-permute-start(bf16[64,3072]{1,0:T(8,128)(2,1)S(1)} %slice.313), channel_id=1, source_target_pairs={{0,2},{1,3},{2,0},{3,1},{4,6},{5,7},{6,4},{7,5},{8,10},{9,11},{10,... | collective-permute-start | bytes 1179656 | tf_op jit(solution)/shard_map/ppermute | solution.py:41
  194.7 12.0 %collective-permute-start.35 = (bf16[64,3072]{1,0:T(8,128)(2,1)S(1)}, bf16[64,3072]{1,0:T(8,128)(2,1)S(1)}, u32[]{:S(2)}, u32[]{:S(2)}) collective-permute-start(bf16[64,3072]{1,0:T(8,128)(2,1)S(1)} %slice.312), channel_id=1, source_target_pairs={{0,1},{1,0},{2,3},{3,2},{4,5},{5,4},{6,7},{7,6},{8,9},{9,8},{10,11... | collective-permute-start | bytes 1179656 | tf_op jit(solution)/shard_map/ppermute | solution.py:38
  196.9 16.7 %collective-permute-start.32 = (bf16[64,3072]{1,0:T(8,128)(2,1)S(1)}, bf16[64,3072]{1,0:T(8,128)(2,1)S(1)}, u32[]{:S(2)}, u32[]{:S(2)}) collective-permute-start(bf16[64,3072]{1,0:T(8,128)(2,1)S(1)} %get-tuple-element.227), channel_id=1, source_target_pairs={{0,2},{1,3},{2,0},{3,1},{4,6},{5,7},{6,4},{7,5},{8,10},{9,11},{10,... | collective-permute-start | bytes 1179656 | tf_op jit(solution)/shard_map/ppermute | solution.py:41
  197.5 17.6 %collective-permute-start.33 = (bf16[64,3072]{1,0:T(8,128)(2,1)S(1)}, bf16[64,3072]{1,0:T(8,128)(2,1)S(1)}, u32[]{:S(2)}, u32[]{:S(2)}) collective-permute-start(bf16[64,3072]{1,0:T(8,128)(2,1)S(1)} %get-tuple-element.229), channel_id=1, source_target_pairs={{0,1},{1,0},{2,3},{3,2},{4,5},{5,4},{6,7},{7,6},{8,9},{9,8},{10,11... | collective-permute-start | bytes 1179656 | tf_op jit(solution)/shard_map/ppermute | solution.py:38
  207.3 14.7 %collective-permute-start.38 = (bf16[64,3072]{1,0:T(8,128)(2,1)S(1)}, bf16[64,3072]{1,0:T(8,128)(2,1)S(1)}, u32[]{:S(2)}, u32[]{:S(2)}) collective-permute-start(bf16[64,3072]{1,0:T(8,128)(2,1)S(1)} %get-tuple-element.231), channel_id=1, source_target_pairs={{0,2},{1,3},{2,0},{3,1},{4,6},{5,7},{6,4},{7,5},{8,10},{9,11},{10,... | collective-permute-start | bytes 1179656 | tf_op jit(solution)/shard_map/ppermute | solution.py:41
  207.9 15.6 %collective-permute-start.39 = (bf16[64,3072]{1,0:T(8,128)(2,1)S(1)}, bf16[64,3072]{1,0:T(8,128)(2,1)S(1)}, u32[]{:S(2)}, u32[]{:S(2)}) collective-permute-start(bf16[64,3072]{1,0:T(8,128)(2,1)S(1)} %get-tuple-element.233), channel_id=1, source_target_pairs={{0,1},{1,0},{2,3},{3,2},{4,5},{5,4},{6,7},{7,6},{8,9},{9,8},{10,11... | collective-permute-start | bytes 1179656 | tf_op jit(solution)/shard_map/ppermute | solution.py:38
  215.2 24.5 %collective-permute-start.36 = (bf16[128,3072]{1,0:T(8,128)(2,1)S(1)}, bf16[128,3072]{1,0:T(8,128)(2,1)S(1)}, u32[]{:S(2)}, u32[]{:S(2)}) collective-permute-start(bf16[128,3072]{1,0:T(8,128)(2,1)S(1)} %constant_dynamic-update-slice_fusion.16), channel_id=1, source_target_pairs={{0,1},{1,0},{2,3},{3,2},{4,5},{5,4},{6,7},{7,6},{8,9},{9,8},{10,11... | collective-permute-start | bytes 2359304 | tf_op jit(solution)/shard_map/ppermute | solution.py:38
  216.8 22.8 %collective-permute-start.37 = (bf16[128,3072]{1,0:T(8,128)(2,1)S(1)}, bf16[128,3072]{1,0:T(8,128)(2,1)S(1)}, u32[]{:S(2)}, u32[]{:S(2)}) collective-permute-start(bf16[128,3072]{1,0:T(8,128)(2,1)S(1)} %constant_dynamic-update-slice_fusion.18), channel_id=1, source_target_pairs={{0,2},{1,3},{2,0},{3,1},{4,6},{5,7},{6,4},{7,5},{8,10},{9,11},{10,... | collective-permute-start | bytes 2359304 | tf_op jit(solution)/shard_map/ppermute | solution.py:41
  243.6 2.6 collective-permute-start.40
  243.6 20.3 %collective-permute-start.42 = (bf16[128,3072]{1,0:T(8,128)(2,1)}, bf16[128,3072]{1,0:T(8,128)(2,1)}, u32[]{:S(2)}, u32[]{:S(2)}) collective-permute-start(bf16[128,3072]{1,0:T(8,128)(2,1)} %constant_dynamic-update-slice_fusion.20), channel_id=1, source_target_pairs={{0,1},{1,0},{2,3},{3,2},{4,5},{5,4},{6,7},{7,6},{8,9},{9,8},{10,11... | collective-permute-start | bytes 2359304 | tf_op jit(solution)/shard_map/ppermute | solution.py:38
  245.1 19.8 %collective-permute-start.43 = (bf16[128,3072]{1,0:T(8,128)(2,1)S(1)}, bf16[128,3072]{1,0:T(8,128)(2,1)}, u32[]{:S(2)}, u32[]{:S(2)}) collective-permute-start(bf16[128,3072]{1,0:T(8,128)(2,1)S(1)} %constant_dynamic-update-slice_fusion.22), channel_id=1, source_target_pairs={{0,2},{1,3},{2,0},{3,1},{4,6},{5,7},{6,4},{7,5},{8,10},{9,11},{10,... | collective-permute-start | bytes 2359304 | tf_op jit(solution)/shard_map/ppermute | solution.py:41
  245.6 30.9 %collective-permute-start.31 = (f32[128,1536]{1,0:T(8,128)}, f32[128,1536]{1,0:T(8,128)S(1)}, u32[]{:S(2)}, u32[]{:S(2)}) collective-permute-start(f32[128,1536]{1,0:T(8,128)} %bitcast.137), channel_id=1, source_target_pairs={{0,4},{4,8},{8,12},{12,0},{1,5},{5,9},{9,13},{13,1},{2,6},{6,10},{... | collective-permute-start | bytes 2359304 | tf_op jit(solution)/shard_map/ppermute | solution.py:47
  276.4 13.5 %collective-permute-start.44 = (f32[4,1,32,1536]{3,2,0,1:T(8,128)S(1)}, f32[4,1,32,1536]{3,2,0,1:T(8,128)S(1)}, u32[]{:S(2)}, u32[]{:S(2)}) collective-permute-start(f32[4,1,32,1536]{3,2,0,1:T(8,128)S(1)} %get-tuple-element.261), channel_id=1, source_target_pairs={{0,16},{16,0},{1,17},{17,1},{2,18},{18,2},{3,19},{19,3},{4,20},{20... | collective-permute-start | bytes 2359304 | tf_op jit(solution)/shard_map/ppermute | solution.py:44
  276.7 45.3 %collective-permute-start.41 = (f32[128,1536]{1,0:T(8,128)S(1)}, f32[128,1536]{1,0:T(8,128)S(1)}, u32[]{:S(2)}, u32[]{:S(2)}) collective-permute-start(f32[128,1536]{1,0:T(8,128)S(1)} %bitcast_add_fusion), channel_id=1, source_target_pairs={{0,8},{4,12},{8,0},{12,4},{1,9},{5,13},{9,1},{13,5},{2,10},{6,14},... | collective-permute-start | bytes 2359304 | tf_op jit(solution)/shard_map/ppermute | solution.py:238
  290.0 32.0 %collective-permute-start.45 = (bf16[128,1536]{1,0:T(8,128)(2,1)S(1)}, bf16[128,1536]{1,0:T(8,128)(2,1)S(1)}, u32[]{:S(2)}, u32[]{:S(2)}) collective-permute-start(bf16[128,1536]{1,0:T(8,128)(2,1)S(1)} %bitcast.144), channel_id=1, source_target_pairs={{0,4},{4,8},{8,12},{12,0},{1,5},{5,9},{9,13},{13,1},{2,6},{6,10},{... | collective-permute-start | bytes 1179656 | tf_op jit(solution)/shard_map/ppermute | solution.py:47
  (43 other events, 364.3 us)
where the time goes:
time: 327 us; the launch traced here: 323 us
  waiting for transfers between devices  121 us (37%)
  matrix products  108 us (33%)
  starting transfers between devices  41 us (13%)
  local copies, waits for them, and re-layouts  34.5 us (11%)
  other arithmetic  14.6 us (4%)
    dot_general x24, matrix products, contract(): lax.dot_general(left, right, (((at_left,), (at_right,)), ((), ())), prefe...  108 us
    ppermute x16, waiting for transfers between devices, swap_x(): return lax.ppermute(a, 'col', [(i, i ^ 1) for i in range(n_col)])  69.4 us
    ppermute x16, waiting for transfers between devices, swap_y(): return lax.ppermute(a, 'col', [(i, i ^ 2) for i in range(n_col)])  24.1 us
    ppermute x1, waiting for transfers between devices, shards(): two = lax.ppermute(two, 'row', [(i, (i + 2) % n_row) for i in range(n_row)])  18.3 us
    ppermute x16, starting transfers between devices, swap_x(): return lax.ppermute(a, 'col', [(i, i ^ 1) for i in range(n_col)])  17.9 us
    ppermute x16, starting transfers between devices, swap_y(): return lax.ppermute(a, 'col', [(i, i ^ 2) for i in range(n_col)])  17 us
    unnamed x92, local copies, waits for them, and re-layouts  15.8 us
    ppermute x5, waiting for transfers between devices, pass_row(): return lax.ppermute(a, 'row', [(i, (i + 1) % n_row) for i in range(n_row)])  8.79 us
  transfers between devices with their start and end apart: 46, of which 21 were waited for; matrix products, arithmetic and copies ran while one was open for 44% of the time, Pallas kernels for 0%

commit v1 on v0

v1 whole, which is shorter than its diff:
```python
import math

import jax
import jax.numpy as jnp
from jax import lax
from jax.experimental import pallas as pl
from jax.experimental.pallas import tpu as pltpu
from jax.sharding import PartitionSpec as P

gelu_const = math.sqrt(2.0 / math.pi)
f32, b16 = jnp.float32, jnp.bfloat16


def gelu_both(value):
    square = value * value
    tangent = jnp.tanh(gelu_const * (value + 0.044715 * square * value))
    half = 0.5 * (1.0 + tangent)
    slope = half + 0.5 * value * (1.0 - tangent * tangent) * gelu_const * (1.0 + 3.0 * 0.044715 * square)
    return value * half, slope


def contract(left, right, at_left, at_right):
    return lax.dot_general(
        left, right, (((at_left,), (at_right,)), ((), ())), preferred_element_type=f32
    )


def call(body, operands, in_specs, outs, out_specs, grid, name, limit=16 * 2**20):
    return pl.pallas_call(
        body,
        grid=grid,
        in_specs=in_specs,
        out_specs=out_specs,
        out_shape=outs,
        compiler_params=pltpu.CompilerParams(vmem_limit_bytes=limit),
        cost_estimate=pl.CostEstimate(flops=1000, bytes_accessed=1000, transcendentals=0),
        name=name,
    )(*operands)


def shape(dims, dtype):
    return jax.ShapeDtypeStruct(dims, dtype)


def tile_of(size, most):
    return max(t for t in range(128, most + 1, 128) if size % t == 0)


whole = pl.BlockSpec(memory_space=pltpu.VMEM)


def first_product(chunk, weight, weight_dim, name):
    tokens = chunk.shape[0]
    hidden = weight.shape[1 - weight_dim]
    half = tokens // 2
    tile = tile_of(hidden, 512)

    def body(chunk_ref, weight_ref, sent_ref, kept_ref):
        for start in range(0, hidden, tile):
            span = pl.ds(start, tile)
            block = weight_ref[:, span] if weight_dim == 0 else weight_ref[span, :]
            total = contract(chunk_ref[...], block, 1, weight_dim)
            kept_ref[:, span] = total[:half]
            sent_ref[:, span] = total[half:].astype(b16)

    return call(
        body, [chunk, weight], [whole] * 2, [shape((half, hidden), b16), shape((half, hidden), f32)], [whole] * 2, (), name
    )


def add_halves(kept_h, came_h, kept_g, came_g):
    tokens, hidden = kept_h.shape
    half = tokens // 2
    tile = tile_of(hidden, 768)

    def body(kh, ch, kg, cg, sent_h, next_h, sent_g, next_g):
        for kept, came, sent, rest in ((kh, ch, sent_h, next_h), (kg, cg, sent_g, next_g)):
            total = kept[...] + came[...].astype(f32)
            rest[...] = total[:half]
            sent[...] = total[half:].astype(b16)

    block = pl.BlockSpec((tokens, tile), lambda i: (0, i))
    part = pl.BlockSpec((half, tile), lambda i: (0, i))
    return call(
        body,
        [kept_h, came_h, kept_g, came_g],
        [block] * 4,
        [shape((half, hidden), b16), shape((half, hidden), f32)] * 2,
        [part] * 4,
        (hidden // tile,),
        "add_halves",
    )


def activate(kept_h, came_h, kept_g, came_g):
    tokens, hidden = kept_h.shape
    tile = tile_of(hidden, 768)

    def body(kh, ch, kg, cg, active_ref, delta_ref):
        value, slope = gelu_both(kh[...] + ch[...].astype(f32))
        active_ref[...] = value.astype(b16)
        delta_ref[...] = ((kg[...] + cg[...].astype(f32)) * slope).astype(b16)

    block = pl.BlockSpec((tokens, tile), lambda i: (0, i))
    return call(
        body, [kept_h, came_h, kept_g, came_g], [block] * 4, [shape((tokens, hidden), b16)] * 2, [block] * 2,
        (hidden // tile,), "activate",
    )


def join_pairs(*arrays):
    rows, columns = arrays[0].shape
    tile = tile_of(columns, 1536)

    def body(*refs):
        for i, out in enumerate(refs[len(arrays):]):
            out[pl.ds(0, rows), :] = refs[2 * i][...]
            out[pl.ds(rows, rows), :] = refs[2 * i + 1][...]

    return call(
        body,
        arrays,
        [pl.BlockSpec((rows, tile), lambda i: (0, i))] * len(arrays),
        [shape((2 * rows, columns), arrays[0].dtype)] * (len(arrays) // 2),
        [pl.BlockSpec((2 * rows, tile), lambda i: (0, i))] * (len(arrays) // 2),
        (columns // tile,),
        "join_pairs",
    )


def input_product(delta, up_weight, core, quarter):
    tokens = delta.shape[0]
    width = up_weight.shape[0]
    tile = tile_of(width, 512)
    half = tokens // 2
    pairs = range(tokens // (2 * quarter))

    def body(*refs):
        delta_ref, weight_ref = refs[:2]
        for start in range(0, width, tile):
            span = pl.ds(start, tile)
            total = contract(delta_ref[...], weight_ref[span, :], 1, 1)
            for i in pairs:
                for other in range(2):
                    rows = total[(2 * i + other) * quarter : (2 * i + other + 1) * quarter]
                    if core is None:
                        refs[2 + other][pl.ds(i * quarter, quarter), span] = rows
                    else:
                        base = pl.multiple_of((refs[2][0] ^ other) * half, half)
                        refs[3][pl.ds(base + i * quarter, quarter), span] = rows

    if core is None:
        return call(body, [delta, up_weight], [whole] * 2, [shape((half, width), f32)] * 2, [whole] * 2, (), "input_product")
    return call(
        body,
        [delta, up_weight, core],
        [whole] * 2 + [pl.BlockSpec(memory_space=pltpu.SMEM)],
        shape((tokens, width), f32),
        whole,
        (),
        "input_product",
    )


def weight_product(lefts, rights, partial, scale, most, name):
    tokens, rows = lefts[0].shape
    columns = rights[0].shape[1]
    tile = tile_of(rows, most)
    count = len(lefts)

    def body(*refs):
        total = contract(refs[0][...], refs[count][...], 0, 0)
        for i in range(1, count):
            total = total + contract(refs[i][...], refs[count + i][...], 0, 0)
        if partial is not None:
            total = total + refs[2 * count][...]
        refs[-1][...] = (total if scale is None else total * scale).astype(refs[-1].dtype)

    block = pl.BlockSpec((tile, columns), lambda i: (i, 0))
    return call(
        body,
        [*lefts, *rights] + ([] if partial is None else [partial]),
        [pl.BlockSpec((tokens, tile), lambda i: (0, i))] * count
        + [pl.BlockSpec((tokens, columns), lambda i: (0, 0))] * count
        + [block] * (partial is not None),
        shape((rows, columns), f32 if scale is None else b16),
        block,
        (rows // tile,),
        name,
        32 * 2**20,
    )


def shards(inputs, up_weight, down_weight, cotangent):
    n_row = lax.axis_size("row")
    replicas = lax.axis_size("dp")
    n_col = lax.axis_size("col")
    assert replicas == 2 and n_col == 4 and n_row % 4 == 0
    rows, width = inputs.shape
    quarter = rows // n_col
    own = lax.axis_index("col")

    def swap_x(a):
        return lax.ppermute(a, "col", [(i, i ^ 1) for i in range(n_col)])

    def swap_y(a):
        return lax.ppermute(a, "col", [(i, i ^ 2) for i in range(n_col)])

    def swap_dp(a):
        return lax.ppermute(a, "dp", [(0, 1), (1, 0)])

    def pass_row(a):
        return lax.ppermute(a, "row", [(i, (i + 1) % n_row) for i in range(n_row)])

    def reorder(a, order):
        blocks = [lax.dynamic_slice_in_dim(a, (own ^ bits) * quarter, quarter, 0) for bits in order]
        return jnp.concatenate(blocks, axis=0)

    x_outer, y_outer = (0, 2, 1, 3), (0, 1, 2, 3)

    def reorder_both():
        def body(own_ref, inputs_ref, cotangent_ref, out_ref):
            for i in range(n_col):
                for ref, order, base in ((inputs_ref, x_outer, 0), (cotangent_ref, y_outer, rows)):
                    source = pl.multiple_of((own_ref[0] ^ order[i]) * quarter, quarter)
                    out_ref[pl.ds(base + i * quarter, quarter), :] = ref[pl.ds(source, quarter), :]

        return pl.pallas_call(
            body,
            in_specs=[pl.BlockSpec(memory_space=pltpu.SMEM), whole, whole],
            out_specs=whole,
            out_shape=jax.ShapeDtypeStruct((2 * rows, width), b16),
            name="reorder",
        )(own.astype(jnp.int32).reshape(1), inputs, cotangent)

    if quarter % 16 == 0:
        moving = reorder_both()
    else:
        moving = jnp.concatenate([reorder(inputs, x_outer), reorder(cotangent, y_outer)], axis=0)

    group = n_row // 4
    tall = group * rows
    work = [{} for _ in range(4)]
    blocks = {0: [moving]}
    aligned = group == 1 and quarter % 16 == 0

    token = ()

    def after(*values):
        tied = lax.optimization_barrier((*values, *token))[: len(values)]
        return tied if len(values) > 1 else tied[0]

    def fetch(at):
        if at > 0:
            blocks[at] = [pass_row(after(blocks[at - 1][-1]))]
        while len(blocks[at]) < group:
            blocks[at].append(pass_row(blocks[at][-1]))

    def mirror(at):
        w = work[at]
        w["mine"] = blocks[at][0] if group == 1 else jnp.concatenate(blocks[at])
        mine = after(w["mine"])
        if at == 1:
            w["other"] = [swap_dp(part) for part in jnp.split(mine, 2)]
        elif at == 0:
            w["other"] = [swap_dp(mine)]
        else:
            pair = lax.all_gather(mine, "dp")
            w["other"] = [lax.dynamic_index_in_dim(pair, 1 - lax.axis_index("dp"), 0, keepdims=False)]

    def arrived(at):
        nonlocal token
        blocks[at][-1] = after(blocks[at][-1])
        token = (*token, blocks[at][-1])

    def build_kernel(mine, *others):
        def body(mine_ref, *refs):
            for part, out in enumerate(refs[-2:]):
                for i in range(n_col):
                    span = pl.ds(part * rows + i * quarter, quarter)
                    out[pl.ds(2 * i * quarter, quarter), :] = mine_ref[span, :]
                    if len(refs) == 3:
                        out[pl.ds((2 * i + 1) * quarter, quarter), :] = refs[0][span, :]
                    else:
                        out[pl.ds((2 * i + 1) * quarter, quarter), :] = refs[part][pl.ds(i * quarter, quarter), :]

        return call(
            body, [mine, *others], [whole] * (1 + len(others)), [shape((2 * rows, width), b16)] * 2, [whole] * 2, (), "build"
        )

    def build(at):
        nonlocal token
        w = work[at]
        mine, *others = after(w["mine"], *w["other"])
        if aligned:
            w["in"], w["cot"] = build_kernel(mine, *others)
        else:
            other = jnp.concatenate(others)
            pair = [a.reshape(group, 2 * n_col, quarter, width).transpose(1, 0, 2, 3) for a in (mine, other)]
            w["in"], w["cot"] = jnp.stack(pair, axis=2).reshape(2, 2 * tall, width)
        token = (w["in"], w["cot"])

    def products(at):
        nonlocal token
        w = work[at]
        w["h_out"], w["h"] = token = first_product(after(w["in"]), up_weight, 0, "hidden_product")
        w["g_out"], w["g"] = token = first_product(after(w["cot"]), down_weight, 1, "delta_act_product")

    def reduce_first(at):
        w = work[at]
        if at < 2:
            w["h_came"], w["g_came"] = swap_x(w["h_out"]), swap_y(w["g_out"])
        else:
            h_out, g_out = after(w["h_out"], w["g_out"])
            w["h_came"], w["g_came"] = swap_x(h_out), swap_y(g_out)

    def reduce_second(at):
        nonlocal token
        w = work[at]
        sent_h, w["h"], sent_g, w["g"] = token = add_halves(*after(w["h"], w["h_came"], w["g"], w["g_came"]))
        w["h_came"], w["g_came"] = swap_y(sent_h), swap_x(sent_g)

    def gather_first(at):
        nonlocal token
        w = work[at]
        w["active"], w["delta"] = token = activate(*after(w["h"], w["h_came"], w["g"], w["g_came"]))
        w["delta_came"], w["active_came"] = swap_y(w["delta"]), swap_x(w["active"])

    def join(at):
        nonlocal token
        w = work[at]
        w["delta"], w["active"] = token = join_pairs(
            *after(w["delta"], w["delta_came"], w["active"], w["active_came"])
        )

    def gather_second(at):
        w = work[at]
        join(at)
        w["delta_came"], w["active_came"] = swap_x(w["delta"]), swap_y(w["active"])

    def add_kernel(dtype, *arrays):
        height = arrays[0].shape[0]
        step = tile_of(height, 128) if height % 128 == 0 else height

        def body(*refs):
            total = refs[0][...]
            for ref in refs[1:-1]:
                total = total + ref[...]
            refs[-1][...] = total.astype(dtype)

        block = pl.BlockSpec((step, tile_of(width, 768)), lambda i, j: (i, j))
        grid = (height // step, width // tile_of(width, 768))
        return call(body, arrays, [block] * len(arrays), shape((height, width), dtype), block, grid, "add")

    def share(at):
        nonlocal token
        w = work[at]
        delta = after(w["delta"])
        if not aligned:
            parts = contract(delta, up_weight, 1, 1).reshape(n_col, group, 2, quarter, width)
            token = (parts,)
            w["part"], w["part_came"] = parts[:, :, 0], swap_dp(parts[:, :, 1])
        elif at < 2:
            parts = input_product(delta, up_weight, lax.axis_index("dp").astype(jnp.int32).reshape(1), quarter)
            token = (parts,)
            w["both"] = lax.psum_scatter(parts, "dp", scatter_dimension=0, tiled=True)
        else:
            w["part"], sent = token = input_product(delta, up_weight, None, quarter)
            w["part_came"] = swap_dp(sent)

    running = None

    def share_sum(at):
        nonlocal token, running
        w = work[at]
        if not aligned:
            part = w["part"] + w["part_came"]
            for step in range(at * group, (at + 1) * group):
                one = part[:, step - at * group].reshape(rows, width)
                if step == 0:
                    w["part"] = one
                else:
                    running = pass_row(one if running is None else running + one)
        elif at < 2:
            w["part"] = w["both"]
            if at == 1:
                running = pass_row(after(w["both"]))
        else:
            total = add_kernel(b16 if at == 3 else f32, *after(w["part"], w["part_came"], running))
            token = (total,)
            running = pass_row(total)

    def grads(chunks, names, partial, most, name):
        nonlocal token
        values = after(*(work[at][k] for k in names for at in chunks))
        count = len(chunks)
        scale = None if partial is None else 1.0 / replicas
        token = (weight_product(values[:count], values[count:], partial, scale, most, name),)
        return token[0]

    fetch(0)
    mirror(0)
    fetch(1)
    build(0)
    products(0)
    reduce_first(0)
    mirror(1)
    fetch(2)
    build(1)
    products(1)
    reduce_first(1)
    reduce_second(0)
    arrived(2)
    reduce_second(1)
    fetch(3)
    mirror(2)
    gather_first(0)
    gather_first(1)
    build(2)
    products(2)
    arrived(3)
    gather_second(0)
    mirror(3)
    gather_second(1)
    build(3)
    products(3)
    join(0)
    reduce_first(2)
    share(0)
    join(1)
    reduce_first(3)
    share(1)
    up_partial = grads((0, 1), ("in", "delta"), None, 256, "up_grad_early")
    reduce_second(2)
    reduce_second(3)
    share_sum(0)
    gather_first(2)
    gather_first(3)
    share_sum(1)
    gather_second(2)
    gather_second(3)
    down_partial = grads((0, 1), ("active", "cot"), None, 512, "down_grad_early")
    join(2)
    share(2)
    join(3)
    share_sum(2)
    share(3)
    up_grad = grads((2, 3), ("in", "delta"), up_partial, 256, "up_grad")
    share_sum(3)
    down_grad = grads((2, 3), ("active", "cot"), down_partial, 512, "down_grad")

    def end_kernel(part, came):
        tile = tile_of(width, 768)

        def body(own_ref, part_ref, came_ref, out_ref):
            total = (part_ref[...] + came_ref[...].astype(f32)).astype(b16)
            for i in range(n_col):
                target = pl.multiple_of((own_ref[0] ^ x_outer[i]) * quarter, quarter)
                out_ref[pl.ds(target, quarter), :] = total[i * quarter : (i + 1) * quarter]

        block = pl.BlockSpec((rows, tile), lambda i: (0, i))
        return call(
            body,
            [own.astype(jnp.int32).reshape(1), part, came],
            [pl.BlockSpec(memory_space=pltpu.SMEM), block, block],
            shape((rows, width), b16),
            block,
            (width // tile,),
            "end",
        )

    if aligned:
        return (end_kernel(work[0]["part"], running), up_grad, down_grad)
    input_grad = work[0]["part"] + running.astype(f32)
    input_grad = input_grad.astype(b16).reshape(2, 2, quarter, width).transpose(1, 0, 2, 3).reshape(rows, width)
    return (reorder(input_grad, y_outer), up_grad, down_grad)


def solution(mesh):
    tokens = P(("dp", "row"), "col")
    up, down = P("col", ("dp", "row")), P(("dp", "row"), "col")
    return jax.shard_map(
        shards,
        mesh=mesh,
        in_specs=(tokens, up, down, tokens),
        out_specs=(tokens, up, down),
        check_vma=False,
    )
```

time: 327 us -> 353 us (1.080)
  Pallas kernels: 2.05 us -> 113 us
  matrix products: 108 us -> 0 us
  local copies, waits for them, and re-layouts: 34.5 us -> 61.6 us
  other arithmetic: 14.6 us -> 0.01 us
  between operations: 1.89 us -> 14.5 us
    pallas_call x0 -> x39, Pallas kernels: none -> 111 us  [call(): pl.pallas_call(body, grid=grid, in_specs=in_specs, out_specs=out_specs, o...]
    dot_general x24 -> x0, matrix products: 108 us -> none  [contract(): lax.dot_general(left, right, (((at_left,), (at_right,)), ((), ())), prefe...]
    unnamed x92 -> x154, local copies, waits for them, and re-layouts: 15.8 us -> 59.2 us
    ppermute x5 -> x6, waiting for transfers between devices: 8.79 us -> 27.8 us  [pass_row(): return lax.ppermute(a, 'row', [(i, (i + 1) % n_row) for i in range(n_row)])]
    ppermute x1 -> x0, waiting for transfers between devices: 18.3 us -> none  [shards(): two = lax.ppermute(two, 'row', [(i, (i + 2) % n_row) for i in range(n_row)])]
    ppermute x16, waiting for transfers between devices: 24.1 us -> 41.1 us  [swap_y(): return lax.ppermute(a, 'col', [(i, i ^ 2) for i in range(n_col)])]
    ppermute x16, waiting for transfers between devices: 69.4 us -> 53.5 us  [swap_x(): return lax.ppermute(a, 'col', [(i, i ^ 1) for i in range(n_col)])]
    concatenate x15 -> x0, local copies, waits for them, and re-layouts: 13.8 us -> none  [the longest x8 7.41 us: join(): jnp.concatenate([own_d, came_d])]
  transfers between devices with their start and end apart: 46 -> 47, of which waited for: 21 -> 22; matrix products, arithmetic and copies ran while one was open for 44% -> 1% of each run, Pallas kernels for 0% -> 29%
where the time goes in v1:
time: 353 us; the launch traced here: 352 us
  waiting for transfers between devices  123 us (35%)
  Pallas kernels  113 us (32%)
  local copies, waits for them, and re-layouts  61.6 us (17%)
  starting transfers between devices  40.6 us (12%)
  between operations  14.5 us (4%)
    pallas_call x39, Pallas kernels, call(): pl.pallas_call(body, grid=grid, in_specs=in_specs, out_specs=out_specs, o...  111 us
    unnamed x154, local copies, waits for them, and re-layouts  59.2 us
    ppermute x16, waiting for transfers between devices, swap_x(): return lax.ppermute(a, 'col', [(i, i ^ 1) for i in range(n_col)])  53.5 us
    ppermute x16, waiting for transfers between devices, swap_y(): return lax.ppermute(a, 'col', [(i, i ^ 2) for i in range(n_col)])  41.1 us
    ppermute x6, waiting for transfers between devices, pass_row(): return lax.ppermute(a, 'row', [(i, (i + 1) % n_row) for i in range(n_row)])  27.8 us
    ppermute x16, starting transfers between devices, swap_y(): return lax.ppermute(a, 'col', [(i, i ^ 2) for i in range(n_col)])  18.3 us
    ppermute x16, starting transfers between devices, swap_x(): return lax.ppermute(a, 'col', [(i, i ^ 1) for i in range(n_col)])  16.6 us
  transfers between devices with their start and end apart: 47, of which 22 were waited for; matrix products, arithmetic and copies ran while one was open for 1% of the time, Pallas kernels for 29%

profile of v1, /device:TPU:0, one launch (start us, length us, event | category | flops | bytes accessed | tf_op | source)
XLA Modules:
  0.0 352.0 jit_solution(16042050980355884666)
XLA Ops:
  7.2 2.0 reorder.1.mine_ref
  9.7 2.6 collective-permute-start.3
  13.6 4.2 %copy-done = bf16[1536,3072]{1,0:T(8,128)(2,1)S(1)} copy-done((bf16[1536,3072]{1,0:T(8,128)(2,1)S(1)}, bf16[1536,3072]{1,0:T(8,128)(2,1)}, u32[]{:S(2)}) %copy-start) | copy-done | bytes 9437208
  17.8 2.6 hidden_product.4
  20.5 3.7 %copy-done.5 = bf16[3072,1536]{1,0:T(8,128)(2,1)S(1)} copy-done((bf16[3072,1536]{1,0:T(8,128)(2,1)S(1)}, bf16[3072,1536]{1,0:T(8,128)(2,1)}, u32[]{:S(2)}) %copy-start.5) | copy-done | bytes 9437208
  24.1 2.6 delta_act_product.4
  26.8 5.9 %collective-permute-done.3.mine_ref = bf16[256,1536]{1,0:T(8,128)(2,1)S(1)} collective-permute-done((bf16[256,1536]{1,0:T(8,128)(2,1)}, bf16[256,1536]{1,0:T(8,128)(2,1)S(1)}, u32[]{:S(2)}, u32[]{:S(2)}) %collective-permute-start.3) | collective-permute-done | bytes 786464 | tf_op jit(solution)/shard_map/ppermute | solution.py:213
  36.6 3.6 %hidden_product.5 = (bf16[128,3072]{1,0:T(8,128)(2,1)}, f32[128,3072]{1,0:T(8,128)S(1)}) custom-call(bf16[256,1536]{1,0:T(8,128)(2,1)S(1)} %get-tuple-element.293.chunk_ref.refs_1_, bf16[1536,3072]{1,0:T(8,128)(2,1)S(1)} %bitcast.9), custom_call_target="tpu_custom_call" | custom-call | flops 1000 | bytes 1000 | tf_op jit(solution)/shard_map/hidden_product/pallas_call | solution.py:29
  40.7 3.5 %delta_act_product.5 = (bf16[128,3072]{1,0:T(8,128)(2,1)}, f32[128,3072]{1,0:T(8,128)S(1)}) custom-call(bf16[256,1536]{1,0:T(8,128)(2,1)S(1)} %get-tuple-element.339.chunk_ref.refs_3_, bf16[3072,1536]{1,0:T(8,128)(2,1)S(1)} %bitcast.15), custom_call_target="tpu_custom_call" | custom-call | flops 1000 | bytes 1000 | tf_op jit(solution)/shard_map/delta_act_product/pallas_call | solution.py:29
  45.5 8.3 %collective-permute-done.1.ch = bf16[128,3072]{1,0:T(8,128)(2,1)S(1)} collective-permute-done((bf16[128,3072]{1,0:T(8,128)(2,1)S(1)}, bf16[128,3072]{1,0:T(8,128)(2,1)S(1)}, u32[]{:S(2)}, u32[]{:S(2)}) %collective-permute-start.1) | collective-permute-done | bytes 786464 | tf_op jit(solution)/shard_map/ppermute | solution.py:204
  55.3 1.9 add_halves.4
  58.9 10.8 %collective-permute-done.8.ch = bf16[128,3072]{1,0:T(8,128)(2,1)S(1)} collective-permute-done((bf16[128,3072]{1,0:T(8,128)(2,1)}, bf16[128,3072]{1,0:T(8,128)(2,1)S(1)}, u32[]{:S(2)}, u32[]{:S(2)}) %collective-permute-start.8) | collective-permute-done | bytes 786464 | tf_op jit(solution)/shard_map/ppermute | solution.py:204
  72.5 2.4 add_halves.5
  83.5 7.2 %collective-permute-done.6.ch = bf16[64,3072]{1,0:T(8,128)(2,1)S(1)} collective-permute-done((bf16[64,3072]{1,0:T(8,128)(2,1)}, bf16[64,3072]{1,0:T(8,128)(2,1)S(1)}, u32[]{:S(2)}, u32[]{:S(2)}) %collective-permute-start.6) | collective-permute-done | bytes 393248 | tf_op jit(solution)/shard_map/ppermute | solution.py:207
  94.5 1.9 activate.4
  100.8 3.5 activate.5
  106.4 4.2 %copy-done.1 = bf16[1536,3072]{1,0:T(8,128)(2,1)S(1)} copy-done((bf16[1536,3072]{1,0:T(8,128)(2,1)S(1)}, bf16[1536,3072]{1,0:T(8,128)(2,1)}, u32[]{:S(2)}) %copy-start.1) | copy-done | bytes 9437208
  110.6 2.6 hidden_product.6
  115.3 3.7 %copy-done.6 = bf16[3072,1536]{1,0:T(8,128)(2,1)S(1)} copy-done((bf16[3072,1536]{1,0:T(8,128)(2,1)S(1)}, bf16[3072,1536]{1,0:T(8,128)(2,1)}, u32[]{:S(2)}) %copy-start.6) | copy-done | bytes 9437208
  119.0 2.6 delta_act_product.6
  123.7 1.9 join_pairs.8
  129.8 8.0 %collective-permute-done.19.refs_3_ = bf16[64,3072]{1,0:T(8,128)(2,1)S(1)} collective-permute-done((bf16[64,3072]{1,0:T(8,128)(2,1)S(1)}, bf16[64,3072]{1,0:T(8,128)(2,1)S(1)}, u32[]{:S(2)}, u32[]{:S(2)}) %collective-permute-start.19) | collective-permute-done | bytes 393248 | tf_op jit(solution)/shard_map/ppermute | solution.py:204
  138.6 2.2 join_pairs.9
  144.1 4.2 %copy-done.2 = bf16[1536,3072]{1,0:T(8,128)(2,1)S(1)} copy-done((bf16[1536,3072]{1,0:T(8,128)(2,1)S(1)}, bf16[1536,3072]{1,0:T(8,128)(2,1)}, u32[]{:S(2)}) %copy-start.2) | copy-done | bytes 9437208
  148.3 2.6 hidden_product.7
  153.0 3.7 %copy-done.7 = bf16[3072,1536]{1,0:T(8,128)(2,1)S(1)} copy-done((bf16[3072,1536]{1,0:T(8,128)(2,1)S(1)}, bf16[3072,1536]{1,0:T(8,128)(2,1)}, u32[]{:S(2)}) %copy-start.7) | copy-done | bytes 9437208
  156.7 2.6 delta_act_product.7
  165.1 3.8 %input_product.4 = f32[256,1536]{1,0:T(8,128)} custom-call(bf16[256,3072]{1,0:T(8,128)(2,1)S(1)} %get-tuple-element.294.refs_0_.refs_2_, bf16[1536,3072]{1,0:T(8,128)(2,1)S(1)} %bitcast.11, s32[1]{0:T(128)} %bitcast.5.refs_2_), custom_call_target="tpu_custom_call" | custom-call | flops 1000 | bytes 1000 | tf_op jit(solution)/shard_map/input_product/pallas_call | solution.py:29
  168.9 2.1 join_pairs.11
  172.2 3.7 %copy-done.3 = bf16[1536,3072]{1,0:T(8,128)(2,1)S(1)} copy-done((bf16[1536,3072]{1,0:T(8,128)(2,1)S(1)}, bf16[1536,3072]{1,0:T(8,128)(2,1)}, u32[]{:S(2)}) %copy-start.3) | copy-done | bytes 9437208
  175.8 2.6 input_product.5
  186.5 9.2 %up_grad_early.1.refs_4_ = f32[1536,3072]{1,0:T(8,128)} custom-call(bf16[256,1536]{1,0:T(8,128)(2,1)S(1)} %copy-done.14, bf16[256,1536]{1,0:T(8,128)(2,1)S(1)} %copy-done.16, bf16[256,3072]{1,0:T(8,128)(2,1)S(1)} %get-tuple-element.294.refs_0_.refs_2_, bf16[256,3072]{1,0:T(8,128)(2,1)S(1)} %get-tuple-element.295.refs_0_.refs_3_), custom_call_target="tpu_custom_call" | custom-call | flops 1000 | bytes 1000 | tf_op jit(solution)/shard_map/up_grad_early/pallas_call | solution.py:29
  195.7 4.9 %collective-permute-done.24.ch = bf16[128,3072]{1,0:T(8,128)(2,1)S(1)} collective-permute-done((bf16[128,3072]{1,0:T(8,128)(2,1)}, bf16[128,3072]{1,0:T(8,128)(2,1)S(1)}, u32[]{:S(2)}, u32[]{:S(2)}) %collective-permute-start.24) | collective-permute-done | bytes 786464 | tf_op jit(solution)/shard_map/ppermute | solution.py:204
  205.1 12.4 %collective-permute-done.22.ch = bf16[128,3072]{1,0:T(8,128)(2,1)S(1)} collective-permute-done((bf16[128,3072]{1,0:T(8,128)(2,1)}, bf16[128,3072]{1,0:T(8,128)(2,1)S(1)}, u32[]{:S(2)}, u32[]{:S(2)}) %collective-permute-start.22) | collective-permute-done | bytes 786464 | tf_op jit(solution)/shard_map/ppermute | solution.py:204
  218.1 1.8 add_halves.7
  222.9 3.6 %collective-permute-done.28.ch = bf16[64,3072]{1,0:T(8,128)(2,1)S(1)} collective-permute-done((bf16[64,3072]{1,0:T(8,128)(2,1)S(1)}, bf16[64,3072]{1,0:T(8,128)(2,1)S(1)}, u32[]{:S(2)}, u32[]{:S(2)}) %collective-permute-start.28) | collective-permute-done | bytes 393248 | tf_op jit(solution)/shard_map/ppermute | solution.py:207
  232.4 6.0 %collective-permute-done.33.refs_3_ = bf16[64,3072]{1,0:T(8,128)(2,1)S(1)} collective-permute-done((bf16[64,3072]{1,0:T(8,128)(2,1)S(1)}, bf16[64,3072]{1,0:T(8,128)(2,1)S(1)}, u32[]{:S(2)}, u32[]{:S(2)}) %collective-permute-start.33) | collective-permute-done | bytes 393248 | tf_op jit(solution)/shard_map/ppermute | solution.py:204
  238.4 2.3 collective-permute-done.32.refs_1_
  244.3 1.9 collective-permute-start.31
  246.2 20.6 %collective-permute-done.30.refs_1_ = bf16[64,3072]{1,0:T(8,128)(2,1)S(1)} collective-permute-done((bf16[64,3072]{1,0:T(8,128)(2,1)S(1)}, bf16[64,3072]{1,0:T(8,128)(2,1)S(1)}, u32[]{:S(2)}, u32[]{:S(2)}) %collective-permute-start.30) | collective-permute-done | bytes 393248 | tf_op jit(solution)/shard_map/ppermute | solution.py:207
  269.8 9.3 %down_grad_early.1.refs_4_ = f32[3072,1536]{1,0:T(8,128)} custom-call(bf16[256,3072]{1,0:T(8,128)(2,1)S(1)} %copy-done.31, bf16[256,3072]{1,0:T(8,128)(2,1)S(1)} %copy-done.33, bf16[256,1536]{1,0:T(8,128)(2,1)S(1)} %copy-done.10, bf16[256,1536]{1,0:T(8,128)(2,1)S(1)} %copy-done.12), custom_call_target="tpu_custom_call" | custom-call | flops 1000 | bytes 1000 | tf_op jit(solution)/shard_map/down_grad_early/pallas_call | solution.py:29
  279.9 3.5 %input_product.6 = (f32[128,1536]{1,0:T(8,128)S(1)}, f32[128,1536]{1,0:T(8,128)}) custom-call(bf16[256,3072]{1,0:T(8,128)(2,1)S(1)} %get-tuple-element.364.refs_0_.refs_2_, bf16[1536,3072]{1,0:T(8,128)(2,1)S(1)} %bitcast.13), custom_call_target="tpu_custom_call" | custom-call | flops 1000 | bytes 1000 | tf_op jit(solution)/shard_map/input_product/pallas_call | solution.py:29
  284.9 2.1 join_pairs.15
  287.0 20.3 %collective-permute-done.39.refs_2_ = f32[128,1536]{1,0:T(8,128)S(1)} collective-permute-done((f32[128,1536]{1,0:T(8,128)}, f32[128,1536]{1,0:T(8,128)S(1)}, u32[]{:S(2)}, u32[]{:S(2)}) %collective-permute-start.39) | collective-permute-done | bytes 786464 | tf_op jit(solution)/shard_map/ppermute | solution.py:213
  308.7 3.7 %copy-done.4 = bf16[1536,3072]{1,0:T(8,128)(2,1)S(1)} copy-done((bf16[1536,3072]{1,0:T(8,128)(2,1)S(1)}, bf16[1536,3072]{1,0:T(8,128)(2,1)}, u32[]{:S(2)}) %copy-start.4) | copy-done | bytes 9437208
  312.4 2.6 input_product.7
  315.1 13.2 %up_grad.1 = bf16[1536,3072]{1,0:T(8,128)(2,1)} custom-call(bf16[256,1536]{1,0:T(8,128)(2,1)S(1)} %copy-done.25, bf16[256,1536]{1,0:T(8,128)(2,1)S(1)} %copy-done.29, bf16[256,3072]{1,0:T(8,128)(2,1)S(1)} %get-tuple-element.364.refs_0_.refs_2_, bf16[256,3072]{1,0:T(8,128)(2,1)S(1)} %get-tuple-element.365.refs_0_.refs_3_, f32[1536,3072]{1,0:T(8,128)} %up_grad_early.1.refs_4_), custom_call_target="tpu_custom_call" | custom-call | flops 1000 | bytes 1000 | tf_op jit(solution)/shard_map/up_grad/pallas_call | solution.py:29
  330.3 13.2 %down_grad.1 = bf16[3072,1536]{1,0:T(8,128)(2,1)} custom-call(bf16[256,3072]{1,0:T(8,128)(2,1)S(1)} %get-tuple-element.369.refs_0_, bf16[256,3072]{1,0:T(8,128)(2,1)S(1)} %get-tuple-element.370.refs_1_, bf16[256,1536]{1,0:T(8,128)(2,1)S(1)} %copy-done.23, bf16[256,1536]{1,0:T(8,128)(2,1)S(1)} %copy-done.27, f32[3072,1536]{1,0:T(8,128)} %down_grad_early.1.refs_4_), custom_call_target="tpu_custom_call" | custom-call | flops 1000 | bytes 1000 | tf_op jit(solution)/shard_map/down_grad/pallas_call | solution.py:29
  (251 shorter events, 89.5 us)
Async XLA Ops:
  7.2 97.9 %all-gather.5.cloned.1.call-start = ((), (), s32[]{:S(2)}) async-start(), calls=%async_computation.4 | async-start | bytes 2359296 | tf_op jit(solution)/shard_map/all_gather | solution.py:268
  9.3 3.0 collective-permute-start
  9.7 23.0 %collective-permute-start.3 = (bf16[256,1536]{1,0:T(8,128)(2,1)}, bf16[256,1536]{1,0:T(8,128)(2,1)S(1)}, u32[]{:S(2)}, u32[]{:S(2)}) collective-permute-start(bf16[256,1536]{1,0:T(8,128)(2,1)} %reorder.1.mine_ref), channel_id=1, source_target_pairs={{0,4},{4,8},{8,12},{12,0},{1,5},{5,9},{9,13},{13,1},{2,6},{6,10},{... | collective-permute-start | bytes 2359304 | tf_op jit(solution)/shard_map/ppermute | solution.py:213
  32.8 3.6 %collective-permute-start.5 = (bf16[128,1536]{1,0:T(8,128)(2,1)S(1)}, bf16[128,1536]{1,0:T(8,128)(2,1)S(1)}, u32[]{:S(2)}, u32[]{:S(2)}) collective-permute-start(bf16[128,1536]{1,0:T(8,128)(2,1)S(1)} %get-tuple-element.373), channel_id=1, source_target_pairs={{0,16},{16,0},{1,17},{17,1},{2,18},{18,2},{3,19},{19,3},{4,20},{20... | collective-permute-start | bytes 1179656 | tf_op jit(solution)/shard_map/ppermute | solution.py:210
  32.9 3.5 collective-permute-start.4
  33.4 20.4 %collective-permute-start.1 = (bf16[128,3072]{1,0:T(8,128)(2,1)S(1)}, bf16[128,3072]{1,0:T(8,128)(2,1)S(1)}, u32[]{:S(2)}, u32[]{:S(2)}) collective-permute-start(bf16[128,3072]{1,0:T(8,128)(2,1)S(1)} %get-tuple-element.194), channel_id=1, source_target_pairs={{0,1},{1,0},{2,3},{3,2},{4,5},{5,4},{6,7},{7,6},{8,9},{9,8},{10,11... | collective-permute-start | bytes 2359304 | tf_op jit(solution)/shard_map/ppermute | solution.py:204
  34.9 24.1 %collective-permute-start.10 = (bf16[256,1536]{1,0:T(8,128)(2,1)S(1)}, bf16[256,1536]{1,0:T(8,128)(2,1)S(1)}, u32[]{:S(2)}, u32[]{:S(2)}) collective-permute-start(bf16[256,1536]{1,0:T(8,128)(2,1)S(1)} %collective-permute-done.3.mine_ref), channel_id=1, source_target_pairs={{0,4},{4,8},{8,12},{12,0},{1,5},{5,9},{9,13},{13,1},{2,6},{6,10},{... | collective-permute-start | bytes 2359304 | tf_op jit(solution)/shard_map/ppermute | solution.py:213
  34.9 20.4 %collective-permute-start.2 = (bf16[128,3072]{1,0:T(8,128)(2,1)S(1)}, bf16[128,3072]{1,0:T(8,128)(2,1)S(1)}, u32[]{:S(2)}, u32[]{:S(2)}) collective-permute-start(bf16[128,3072]{1,0:T(8,128)(2,1)S(1)} %get-tuple-element.197), channel_id=1, source_target_pairs={{0,2},{1,3},{2,0},{3,1},{4,6},{5,7},{6,4},{7,5},{8,10},{9,11},{10,... | collective-permute-start | bytes 2359304 | tf_op jit(solution)/shard_map/ppermute | solution.py:207
  40.1 29.6 %collective-permute-start.8 = (bf16[128,3072]{1,0:T(8,128)(2,1)}, bf16[128,3072]{1,0:T(8,128)(2,1)S(1)}, u32[]{:S(2)}, u32[]{:S(2)}) collective-permute-start(bf16[128,3072]{1,0:T(8,128)(2,1)} %get-tuple-element.205), channel_id=1, source_target_pairs={{0,1},{1,0},{2,3},{3,2},{4,5},{5,4},{6,7},{7,6},{8,9},{9,8},{10,11... | collective-permute-start | bytes 2359304 | tf_op jit(solution)/shard_map/ppermute | solution.py:204
  44.2 26.8 %collective-permute-start.9 = (bf16[128,3072]{1,0:T(8,128)(2,1)}, bf16[128,3072]{1,0:T(8,128)(2,1)}, u32[]{:S(2)}, u32[]{:S(2)}) collective-permute-start(bf16[128,3072]{1,0:T(8,128)(2,1)} %get-tuple-element.208), channel_id=1, source_target_pairs={{0,2},{1,3},{2,0},{3,1},{4,6},{5,7},{6,4},{7,5},{8,10},{9,11},{10,... | collective-permute-start | bytes 2359304 | tf_op jit(solution)/shard_map/ppermute | solution.py:207
  78.3 64.4 %all-gather.7.cloned.1.call-start = ((), (), s32[]{:S(2)}) async-start(), calls=%async_computation.5 | async-start | bytes 2359296 | tf_op jit(solution)/shard_map/all_gather | solution.py:268
  78.4 12.3 %collective-permute-start.6 = (bf16[64,3072]{1,0:T(8,128)(2,1)}, bf16[64,3072]{1,0:T(8,128)(2,1)S(1)}, u32[]{:S(2)}, u32[]{:S(2)}) collective-permute-start(bf16[64,3072]{1,0:T(8,128)(2,1)} %get-tuple-element.215), channel_id=1, source_target_pairs={{0,2},{1,3},{2,0},{3,1},{4,6},{5,7},{6,4},{7,5},{8,10},{9,11},{10,... | collective-permute-start | bytes 1179656 | tf_op jit(solution)/shard_map/ppermute | solution.py:207
  80.0 12.3 %collective-permute-start.7 = (bf16[64,3072]{1,0:T(8,128)(2,1)}, bf16[64,3072]{1,0:T(8,128)(2,1)S(1)}, u32[]{:S(2)}, u32[]{:S(2)}) collective-permute-start(bf16[64,3072]{1,0:T(8,128)(2,1)} %get-tuple-element.217), channel_id=1, source_target_pairs={{0,1},{1,0},{2,3},{3,2},{4,5},{5,4},{6,7},{7,6},{8,9},{9,8},{10,11... | collective-permute-start | bytes 1179656 | tf_op jit(solution)/shard_map/ppermute | solution.py:204
  80.5 43.1 %collective-permute-start.15 = (bf16[256,1536]{1,0:T(8,128)(2,1)}, bf16[256,1536]{1,0:T(8,128)(2,1)S(1)}, u32[]{:S(2)}, u32[]{:S(2)}) collective-permute-start(bf16[256,1536]{1,0:T(8,128)(2,1)} %copy-done.17), channel_id=1, source_target_pairs={{0,4},{4,8},{8,12},{12,0},{1,5},{5,9},{9,13},{13,1},{2,6},{6,10},{... | collective-permute-start | bytes 2359304 | tf_op jit(solution)/shard_map/ppermute | solution.py:213
  81.5 17.6 %collective-permute-start.13 = (bf16[64,3072]{1,0:T(8,128)(2,1)}, bf16[64,3072]{1,0:T(8,128)(2,1)S(1)}, u32[]{:S(2)}, u32[]{:S(2)}) collective-permute-start(bf16[64,3072]{1,0:T(8,128)(2,1)} %copy-done.64), channel_id=1, source_target_pairs={{0,2},{1,3},{2,0},{3,1},{4,6},{5,7},{6,4},{7,5},{8,10},{9,11},{10,... | collective-permute-start | bytes 1179656 | tf_op jit(solution)/shard_map/ppermute | solution.py:207
  82.0 18.7 %collective-permute-start.14 = (bf16[64,3072]{1,0:T(8,128)(2,1)}, bf16[64,3072]{1,0:T(8,128)(2,1)}, u32[]{:S(2)}, u32[]{:S(2)}) collective-permute-start(bf16[64,3072]{1,0:T(8,128)(2,1)} %copy-done.63), channel_id=1, source_target_pairs={{0,1},{1,0},{2,3},{3,2},{4,5},{5,4},{6,7},{7,6},{8,9},{9,8},{10,11... | collective-permute-start | bytes 1179656 | tf_op jit(solution)/shard_map/ppermute | solution.py:204
  96.5 27.2 %collective-permute-start.11 = (bf16[64,3072]{1,0:T(8,128)(2,1)}, bf16[64,3072]{1,0:T(8,128)(2,1)}, u32[]{:S(2)}, u32[]{:S(2)}) collective-permute-start(bf16[64,3072]{1,0:T(8,128)(2,1)} %get-tuple-element.251.refs_0_), channel_id=1, source_target_pairs={{0,2},{1,3},{2,0},{3,1},{4,6},{5,7},{6,4},{7,5},{8,10},{9,11},{10,... | collective-permute-start | bytes 1179656 | tf_op jit(solution)/shard_map/ppermute | solution.py:207
  97.0 26.7 %collective-permute-start.12 = (bf16[64,3072]{1,0:T(8,128)(2,1)}, bf16[64,3072]{1,0:T(8,128)(2,1)}, u32[]{:S(2)}, u32[]{:S(2)}) collective-permute-start(bf16[64,3072]{1,0:T(8,128)(2,1)} %get-tuple-element.253.refs_2_), channel_id=1, source_target_pairs={{0,1},{1,0},{2,3},{3,2},{4,5},{5,4},{6,7},{7,6},{8,9},{9,8},{10,11... | collective-permute-start | bytes 1179656 | tf_op jit(solution)/shard_map/ppermute | solution.py:204
  125.6 158.7 %reduce-scatter.5.cloned.1.call-start = ((), (), s32[]{:S(2)}) async-start(), calls=%async_computation.3 | async-start | bytes 2359296 | tf_op jit(solution)/shard_map/reduce_scatter | solution.py:366
  125.7 12.1 %collective-permute-start.19 = (bf16[64,3072]{1,0:T(8,128)(2,1)S(1)}, bf16[64,3072]{1,0:T(8,128)(2,1)S(1)}, u32[]{:S(2)}, u32[]{:S(2)}) collective-permute-start(bf16[64,3072]{1,0:T(8,128)(2,1)S(1)} %copy-done.58), channel_id=1, source_target_pairs={{0,1},{1,0},{2,3},{3,2},{4,5},{5,4},{6,7},{7,6},{8,9},{9,8},{10,11... | collective-permute-start | bytes 1179656 | tf_op jit(solution)/shard_map/ppermute | solution.py:204
  126.3 12.3 %collective-permute-start.18 = (bf16[64,3072]{1,0:T(8,128)(2,1)}, bf16[64,3072]{1,0:T(8,128)(2,1)S(1)}, u32[]{:S(2)}, u32[]{:S(2)}) collective-permute-start(bf16[64,3072]{1,0:T(8,128)(2,1)} %get-tuple-element.258.refs_0_), channel_id=1, source_target_pairs={{0,2},{1,3},{2,0},{3,1},{4,6},{5,7},{6,4},{7,5},{8,10},{9,11},{10,... | collective-permute-start | bytes 1179656 | tf_op jit(solution)/shard_map/ppermute | solution.py:207
  126.8 33.4 %collective-permute-start.16 = (bf16[128,3072]{1,0:T(8,128)(2,1)S(1)}, bf16[128,3072]{1,0:T(8,128)(2,1)S(1)}, u32[]{:S(2)}, u32[]{:S(2)}) collective-permute-start(bf16[128,3072]{1,0:T(8,128)(2,1)S(1)} %get-tuple-element.274.refs_0_), channel_id=1, source_target_pairs={{0,1},{1,0},{2,3},{3,2},{4,5},{5,4},{6,7},{7,6},{8,9},{9,8},{10,11... | collective-permute-start | bytes 2359304 | tf_op jit(solution)/shard_map/ppermute | solution.py:204
  128.3 32.9 %collective-permute-start.17 = (bf16[128,3072]{1,0:T(8,128)(2,1)S(1)}, bf16[128,3072]{1,0:T(8,128)(2,1)}, u32[]{:S(2)}, u32[]{:S(2)}) collective-permute-start(bf16[128,3072]{1,0:T(8,128)(2,1)S(1)} %get-tuple-element.276.refs_2_), channel_id=1, source_target_pairs={{0,2},{1,3},{2,0},{3,1},{4,6},{5,7},{6,4},{7,5},{8,10},{9,11},{10,... | collective-permute-start | bytes 2359304 | tf_op jit(solution)/shard_map/ppermute | solution.py:207
  140.7 28.2 %collective-permute-start.20 = (bf16[128,3072]{1,0:T(8,128)(2,1)}, bf16[128,3072]{1,0:T(8,128)(2,1)}, u32[]{:S(2)}, u32[]{:S(2)}) collective-permute-start(bf16[128,3072]{1,0:T(8,128)(2,1)} %get-tuple-element.281.refs_0_), channel_id=1, source_target_pairs={{0,1},{1,0},{2,3},{3,2},{4,5},{5,4},{6,7},{7,6},{8,9},{9,8},{10,11... | collective-permute-start | bytes 2359304 | tf_op jit(solution)/shard_map/ppermute | solution.py:204
  142.2 26.7 %collective-permute-start.21 = (bf16[128,3072]{1,0:T(8,128)(2,1)}, bf16[128,3072]{1,0:T(8,128)(2,1)}, u32[]{:S(2)}, u32[]{:S(2)}) collective-permute-start(bf16[128,3072]{1,0:T(8,128)(2,1)} %get-tuple-element.283.refs_2_), channel_id=1, source_target_pairs={{0,2},{1,3},{2,0},{3,1},{4,6},{5,7},{6,4},{7,5},{8,10},{9,11},{10,... | collective-permute-start | bytes 2359304 | tf_op jit(solution)/shard_map/ppermute | solution.py:207
  179.6 163.9 %reduce-scatter.3.cloned.1.call-start = ((), (), s32[]{:S(2)}) async-start(), calls=%async_computation.2 | async-start | bytes 2359296 | tf_op jit(solution)/shard_map/reduce_scatter | solution.py:366
  179.9 20.8 %collective-permute-start.24 = (bf16[128,3072]{1,0:T(8,128)(2,1)}, bf16[128,3072]{1,0:T(8,128)(2,1)S(1)}, u32[]{:S(2)}, u32[]{:S(2)}) collective-permute-start(bf16[128,3072]{1,0:T(8,128)(2,1)} %copy-done.59), channel_id=1, source_target_pairs={{0,1},{1,0},{2,3},{3,2},{4,5},{5,4},{6,7},{7,6},{8,9},{9,8},{10,11... | collective-permute-start | bytes 2359304 | tf_op jit(solution)/shard_map/ppermute | solution.py:204
  180.5 20.7 %collective-permute-start.25 = (bf16[128,3072]{1,0:T(8,128)(2,1)}, bf16[128,3072]{1,0:T(8,128)(2,1)S(1)}, u32[]{:S(2)}, u32[]{:S(2)}) collective-permute-start(bf16[128,3072]{1,0:T(8,128)(2,1)} %copy-done.60), channel_id=1, source_target_pairs={{0,2},{1,3},{2,0},{3,1},{4,6},{5,7},{6,4},{7,5},{8,10},{9,11},{10,... | collective-permute-start | bytes 2359304 | tf_op jit(solution)/shard_map/ppermute | solution.py:207
  182.0 35.5 %collective-permute-start.22 = (bf16[128,3072]{1,0:T(8,128)(2,1)}, bf16[128,3072]{1,0:T(8,128)(2,1)S(1)}, u32[]{:S(2)}, u32[]{:S(2)}) collective-permute-start(bf16[128,3072]{1,0:T(8,128)(2,1)} %copy-done.61), channel_id=1, source_target_pairs={{0,1},{1,0},{2,3},{3,2},{4,5},{5,4},{6,7},{7,6},{8,9},{9,8},{10,11... | collective-permute-start | bytes 2359304 | tf_op jit(solution)/shard_map/ppermute | solution.py:204
  183.5 34.5 %collective-permute-start.23 = (bf16[128,3072]{1,0:T(8,128)(2,1)}, bf16[128,3072]{1,0:T(8,128)(2,1)S(1)}, u32[]{:S(2)}, u32[]{:S(2)}) collective-permute-start(bf16[128,3072]{1,0:T(8,128)(2,1)} %copy-done.62), channel_id=1, source_target_pairs={{0,2},{1,3},{2,0},{3,1},{4,6},{5,7},{6,4},{7,5},{8,10},{9,11},{10,... | collective-permute-start | bytes 2359304 | tf_op jit(solution)/shard_map/ppermute | solution.py:207
  202.1 24.4 %collective-permute-start.28 = (bf16[64,3072]{1,0:T(8,128)(2,1)S(1)}, bf16[64,3072]{1,0:T(8,128)(2,1)S(1)}, u32[]{:S(2)}, u32[]{:S(2)}) collective-permute-start(bf16[64,3072]{1,0:T(8,128)(2,1)S(1)} %get-tuple-element.300), channel_id=1, source_target_pairs={{0,2},{1,3},{2,0},{3,1},{4,6},{5,7},{6,4},{7,5},{8,10},{9,11},{10,... | collective-permute-start | bytes 1179656 | tf_op jit(solution)/shard_map/ppermute | solution.py:207
  203.7 22.8 %collective-permute-start.29 = (bf16[64,3072]{1,0:T(8,128)(2,1)S(1)}, bf16[64,3072]{1,0:T(8,128)(2,1)S(1)}, u32[]{:S(2)}, u32[]{:S(2)}) collective-permute-start(bf16[64,3072]{1,0:T(8,128)(2,1)S(1)} %get-tuple-element.302), channel_id=1, source_target_pairs={{0,1},{1,0},{2,3},{3,2},{4,5},{5,4},{6,7},{7,6},{8,9},{9,8},{10,11... | collective-permute-start | bytes 1179656 | tf_op jit(solution)/shard_map/ppermute | solution.py:204
  219.9 11.6 %collective-permute-start.26 = (bf16[64,3072]{1,0:T(8,128)(2,1)}, bf16[64,3072]{1,0:T(8,128)(2,1)S(1)}, u32[]{:S(2)}, u32[]{:S(2)}) collective-permute-start(bf16[64,3072]{1,0:T(8,128)(2,1)} %get-tuple-element.309), channel_id=1, source_target_pairs={{0,2},{1,3},{2,0},{3,1},{4,6},{5,7},{6,4},{7,5},{8,10},{9,11},{10,... | collective-permute-start | bytes 1179656 | tf_op jit(solution)/shard_map/ppermute | solution.py:207
  221.4 10.0 %collective-permute-start.27 = (bf16[64,3072]{1,0:T(8,128)(2,1)}, bf16[64,3072]{1,0:T(8,128)(2,1)S(1)}, u32[]{:S(2)}, u32[]{:S(2)}) collective-permute-start(bf16[64,3072]{1,0:T(8,128)(2,1)} %get-tuple-element.311), channel_id=1, source_target_pairs={{0,1},{1,0},{2,3},{3,2},{4,5},{5,4},{6,7},{7,6},{8,9},{9,8},{10,11... | collective-permute-start | bytes 1179656 | tf_op jit(solution)/shard_map/ppermute | solution.py:204
  227.4 11.0 %collective-permute-start.33 = (bf16[64,3072]{1,0:T(8,128)(2,1)S(1)}, bf16[64,3072]{1,0:T(8,128)(2,1)S(1)}, u32[]{:S(2)}, u32[]{:S(2)}) collective-permute-start(bf16[64,3072]{1,0:T(8,128)(2,1)S(1)} %get-tuple-element.326.refs_2_), channel_id=1, source_target_pairs={{0,1},{1,0},{2,3},{3,2},{4,5},{5,4},{6,7},{7,6},{8,9},{9,8},{10,11... | collective-permute-start | bytes 1179656 | tf_op jit(solution)/shard_map/ppermute | solution.py:204
  228.6 12.1 %collective-permute-start.32 = (bf16[64,3072]{1,0:T(8,128)(2,1)S(1)}, bf16[64,3072]{1,0:T(8,128)(2,1)}, u32[]{:S(2)}, u32[]{:S(2)}) collective-permute-start(bf16[64,3072]{1,0:T(8,128)(2,1)S(1)} %get-tuple-element.324.refs_0_), channel_id=1, source_target_pairs={{0,2},{1,3},{2,0},{3,1},{4,6},{5,7},{6,4},{7,5},{8,10},{9,11},{10,... | collective-permute-start | bytes 1179656 | tf_op jit(solution)/shard_map/ppermute | solution.py:207
  231.5 38.4 %copy-start.33 = (bf16[256,3072]{1,0:T(8,128)(2,1)S(1)}, bf16[256,3072]{1,0:T(8,128)(2,1)}, u32[]{:S(2)}) copy-start(bf16[256,3072]{1,0:T(8,128)(2,1)} %copy-done.32) | copy-start | bytes 4718596
  242.1 37.1 %collective-permute-start.36 = (bf16[128,3072]{1,0:T(8,128)(2,1)S(1)}, bf16[128,3072]{1,0:T(8,128)(2,1)S(1)}, u32[]{:S(2)}, u32[]{:S(2)}) collective-permute-start(bf16[128,3072]{1,0:T(8,128)(2,1)S(1)} %get-tuple-element.340.refs_0_), channel_id=1, source_target_pairs={{0,1},{1,0},{2,3},{3,2},{4,5},{5,4},{6,7},{7,6},{8,9},{9,8},{10,11... | collective-permute-start | bytes 2359304 | tf_op jit(solution)/shard_map/ppermute | solution.py:204
  242.3 36.8 %collective-permute-start.37 = (bf16[128,3072]{1,0:T(8,128)(2,1)S(1)}, bf16[128,3072]{1,0:T(8,128)(2,1)S(1)}, u32[]{:S(2)}, u32[]{:S(2)}) collective-permute-start(bf16[128,3072]{1,0:T(8,128)(2,1)S(1)} %get-tuple-element.342.refs_2_), channel_id=1, source_target_pairs={{0,2},{1,3},{2,0},{3,1},{4,6},{5,7},{6,4},{7,5},{8,10},{9,11},{10,... | collective-permute-start | bytes 2359304 | tf_op jit(solution)/shard_map/ppermute | solution.py:207
  243.9 22.9 %collective-permute-start.30 = (bf16[64,3072]{1,0:T(8,128)(2,1)S(1)}, bf16[64,3072]{1,0:T(8,128)(2,1)S(1)}, u32[]{:S(2)}, u32[]{:S(2)}) collective-permute-start(bf16[64,3072]{1,0:T(8,128)(2,1)S(1)} %get-tuple-element.330.refs_0_), channel_id=1, source_target_pairs={{0,2},{1,3},{2,0},{3,1},{4,6},{5,7},{6,4},{7,5},{8,10},{9,11},{10,... | collective-permute-start | bytes 1179656 | tf_op jit(solution)/shard_map/ppermute | solution.py:207
  244.3 22.5 %collective-permute-start.31 = (bf16[64,3072]{1,0:T(8,128)(2,1)S(1)}, bf16[64,3072]{1,0:T(8,128)(2,1)S(1)}, u32[]{:S(2)}, u32[]{:S(2)}) collective-permute-start(bf16[64,3072]{1,0:T(8,128)(2,1)S(1)} %get-tuple-element.332.refs_2_), channel_id=1, source_target_pairs={{0,1},{1,0},{2,3},{3,2},{4,5},{5,4},{6,7},{7,6},{8,9},{9,8},{10,11... | collective-permute-start | bytes 1179656 | tf_op jit(solution)/shard_map/ppermute | solution.py:204
  268.1 16.7 %collective-permute-start.34 = (bf16[128,3072]{1,0:T(8,128)(2,1)}, bf16[128,3072]{1,0:T(8,128)(2,1)}, u32[]{:S(2)}, u32[]{:S(2)}) collective-permute-start(bf16[128,3072]{1,0:T(8,128)(2,1)} %get-tuple-element.349.refs_0_), channel_id=1, source_target_pairs={{0,1},{1,0},{2,3},{3,2},{4,5},{5,4},{6,7},{7,6},{8,9},{9,8},{10,11... | collective-permute-start | bytes 2359304 | tf_op jit(solution)/shard_map/ppermute | solution.py:204
  268.3 16.6 %collective-permute-start.35 = (bf16[128,3072]{1,0:T(8,128)(2,1)}, bf16[128,3072]{1,0:T(8,128)(2,1)}, u32[]{:S(2)}, u32[]{:S(2)}) collective-permute-start(bf16[128,3072]{1,0:T(8,128)(2,1)} %get-tuple-element.351.refs_2_), channel_id=1, source_target_pairs={{0,2},{1,3},{2,0},{3,1},{4,6},{5,7},{6,4},{7,5},{8,10},{9,11},{10,... | collective-permute-start | bytes 2359304 | tf_op jit(solution)/shard_map/ppermute | solution.py:207
  284.3 2.7 collective-permute-start.38
  284.3 23.0 %collective-permute-start.39 = (f32[128,1536]{1,0:T(8,128)}, f32[128,1536]{1,0:T(8,128)S(1)}, u32[]{:S(2)}, u32[]{:S(2)}) collective-permute-start(f32[128,1536]{1,0:T(8,128)} %reduce-scatter.5.cloned.1.call-done), channel_id=1, source_target_pairs={{0,4},{4,8},{8,12},{12,0},{1,5},{5,9},{9,13},{13,1},{2,6},{6,10},{... | collective-permute-start | bytes 2359304 | tf_op jit(solution)/shard_map/ppermute | solution.py:213
  308.6 21.2 %collective-permute-start.41 = (f32[128,1536]{1,0:T(8,128)S(1)}, f32[128,1536]{1,0:T(8,128)S(1)}, u32[]{:S(2)}, u32[]{:S(2)}) collective-permute-start(f32[128,1536]{1,0:T(8,128)S(1)} %add.15), channel_id=1, source_target_pairs={{0,4},{4,8},{8,12},{12,0},{1,5},{5,9},{9,13},{13,1},{2,6},{6,10},{... | collective-permute-start | bytes 2359304 | tf_op jit(solution)/shard_map/ppermute | solution.py:213
  315.0 14.8 %collective-permute-start.40 = (f32[128,1536]{1,0:T(8,128)S(1)}, f32[128,1536]{1,0:T(8,128)S(1)}, u32[]{:S(2)}, u32[]{:S(2)}) collective-permute-start(f32[128,1536]{1,0:T(8,128)S(1)} %get-tuple-element.361), channel_id=1, source_target_pairs={{0,16},{16,0},{1,17},{17,1},{2,18},{18,2},{3,19},{19,3},{4,20},{20... | collective-permute-start | bytes 2359304 | tf_op jit(solution)/shard_map/ppermute | solution.py:210
  330.2 13.3 %collective-permute-start.42 = (bf16[128,1536]{1,0:T(8,128)(2,1)S(1)}, bf16[128,1536]{1,0:T(8,128)(2,1)S(1)}, u32[]{:S(2)}, u32[]{:S(2)}) collective-permute-start(bf16[128,1536]{1,0:T(8,128)(2,1)S(1)} %add.16), channel_id=1, source_target_pairs={{0,4},{4,8},{8,12},{12,0},{1,5},{5,9},{9,13},{13,1},{2,6},{6,10},{... | collective-permute-start | bytes 1179656 | tf_op jit(solution)/shard_map/ppermute | solution.py:213
  (76 other events, 578.0 us)
Sparse Core Ops, SparseCore 0:
  78.5 10.0 all-gather.4
  125.7 9.1 all-gather.6
  179.8 9.2 reduce-scatter.4
  230.5 8.5 reduce-scatter.2
